TPU v7x, 1024 devices: a whole 4x8x16 slice. The times are simulated.
1024 devices in a mesh: node: 128 (over z_lo, y, core), dev: 8 (over x, z_hi).
Axes of the slice: x: 4, y: 8, z: 16 (z_hi: 2, z_lo: 8; z = z_hi * 8 + z_lo), core: 2. Of those that a mesh axis runs over, the one named last changes fastest.
Arguments:
- coarse_state: float32 [5, 2048, 2048], P(None, 'node', 'dev'), as said below
- fine_state: float32 [6144, 5, 512], P(('node', 'dev')), as said below
- fine_anchor: int32 [1024, 2, 3], P(('node', 'dev')), may hold values from 2 to 10, as said below
- fine_owner: int32 [1024, 2, 2], P(('node', 'dev')), may hold values from 0 to 5, as said below
Outputs:
- coarse_new: float32 [5, 2048, 2048], P(None, 'node', 'dev')
- fine_new: float32 [6144, 5, 512], P(('node', 'dev'))
Inputs may be any that keep to these rules, and one draw needn't show every extreme that they name: `coarse_state`: density in [0.5, 2], every velocity component in [-0.3, 0.3], pressure in [0.5, 2] in every cell, with E = p / 0.4 + rho |u|^2 / 2. `fine_state`: same law as coarse_state in every slot; slots that hold no fine box are not read. `fine_anchor`: z and y anchors lie in [2, 10]; the x anchor of fine box 0 lies in [2, 3], that of fine box 1 in [10, 10]. Fine regions lie 2 or more coarse cells inside their box and never touch each other. `fine_owner`: k < 4 and s < 6; no two fine boxes share a slot of a device; every device holds at most 6 fine boxes and in every draw some devices hold exactly 6, while the mean is 2; both fine boxes of one coarse box may have the same k.
All inputs are finite; a program needn't handle non-finite values.
Results may differ from a plain program's by a relative error of at most 0.0003.
Values sent between devices are 32-bit elements; how exact they have to be, the bound alone decides.
No kernel may reach another device: no remote copies, remote signals or barrier semaphores. Data moves between devices by JAX's collectives and lax.ppermute only.
A program may use at most 64 MiB of HBM per device.

v0:
```python
import jax
import jax.numpy as jnp
from jax import lax
from jax.sharding import PartitionSpec as P

F = 8
FPC = 2
SPAN = 4
CAP = 6


GAMMA = 1.4
RATIO = 0.06
SLAB_CELLS = 4


def passed_along(value, axis, steps):
    count = lax.axis_size(axis)
    pairs = [(source, (source + steps) % count) for source in range(count)]
    return lax.ppermute(value, axis, pairs)


def with_halo(array, sides, width):
    for axis, dim in sides:
        size, length = (lax.axis_size(axis), array.shape[dim])
        up = [(i, (i + 1) % size) for i in range(size)]
        down = [(j, i) for i, j in up]
        last = lax.slice_in_dim(array, length - width, length, axis=dim)
        initial = lax.slice_in_dim(array, 0, width, axis=dim)
        before = lax.ppermute(last, axis, up)
        after = lax.ppermute(initial, axis, down)
        array = jnp.concatenate([before, array, after], axis=dim)
    return array


def primitives(conserved, member):
    density = conserved[0]
    velocity = conserved[member] / density
    kinetic = (
        0.5
        * (conserved[1] * conserved[1] + conserved[2] * conserved[2] + conserved[3] * conserved[3])
        / density
    )
    pressure = (GAMMA - 1.0) * (conserved[4] - kinetic)
    sound_speed = jnp.sqrt(GAMMA * pressure / density)
    return (velocity, pressure, sound_speed)


def physical(conserved, velocity, pressure, member):
    pieces = []
    for position in range(5):
        entry_term = conserved[position] * velocity
        if position == member:
            entry_term = entry_term + pressure
        if position == 4:
            entry_term = entry_term + pressure * velocity
        pieces.append(entry_term)
    return jnp.stack(pieces)


def rusanov(lower_cells, upper_cells, member):
    velocity_low, pressure_low, sound_low = primitives(lower_cells, member)
    velocity_up, pressure_up, sound_up = primitives(upper_cells, member)
    wave_speed = jnp.maximum(jnp.abs(velocity_low) + sound_low, jnp.abs(velocity_up) + sound_up)
    average = 0.5 * (
        physical(lower_cells, velocity_low, pressure_low, member)
        + physical(upper_cells, velocity_up, pressure_up, member)
    )
    return average - 0.5 * wave_speed * (upper_cells - lower_cells)


def advance(padded):
    interior = padded[:, 1:-1, 1:-1, 1:-1]
    flux_z = rusanov(padded[:, :-1, 1:-1, 1:-1], padded[:, 1:, 1:-1, 1:-1], 3)
    flux_x = rusanov(padded[:, 1:-1, :-1, 1:-1], padded[:, 1:-1, 1:, 1:-1], 1)
    flux_y = rusanov(padded[:, 1:-1, 1:-1, :-1], padded[:, 1:-1, 1:-1, 1:], 2)
    change = (
        flux_z[:, 1:]
        - flux_z[:, :-1]
        + (flux_x[:, :, 1:] - flux_x[:, :, :-1])
        + (flux_y[:, :, :, 1:] - flux_y[:, :, :, :-1])
    )
    return (interior - RATIO * change, flux_z, flux_x, flux_y)


def slab_advance(padded):
    inner_edge = padded.shape[1] - 2
    slab_count = inner_edge // SLAB_CELLS

    def one_slab(slab_index):
        start = slab_index * SLAB_CELLS
        piece = lax.dynamic_slice_in_dim(padded, start, SLAB_CELLS + 2, 1)
        return advance(piece)

    stepped_s, flux_z_s, flux_x_s, flux_y_s = lax.map(
        one_slab, jnp.arange(slab_count, dtype=jnp.int32)
    )

    def join(stacked):
        moved = jnp.moveaxis(stacked, 0, 1)
        return moved.reshape((5, slab_count * stacked.shape[2]) + stacked.shape[3:])

    stepped = join(stepped_s)
    flux_x = join(flux_x_s)
    flux_y = join(flux_y_s)
    flux_z = jnp.concatenate(
        [join(flux_z_s[:, :, :SLAB_CELLS]), flux_z_s[-1][:, SLAB_CELLS:]], axis=1
    )
    return (stepped, flux_z, flux_x, flux_y)


def minmod(lower_diff, upper_diff):
    smaller = jnp.where(jnp.abs(lower_diff) < jnp.abs(upper_diff), lower_diff, upper_diff)
    return jnp.where(lower_diff * upper_diff > 0.0, smaller, 0.0)


def refine_all(field):
    return jnp.repeat(jnp.repeat(jnp.repeat(field, 2, axis=1), 2, axis=2), 2, axis=3)


def interpolate(block):
    center = block[:, 1:-1, 1:-1, 1:-1]
    slope_z = minmod(center - block[:, :-2, 1:-1, 1:-1], block[:, 2:, 1:-1, 1:-1] - center)
    slope_x = minmod(center - block[:, 1:-1, :-2, 1:-1], block[:, 1:-1, 2:, 1:-1] - center)
    slope_y = minmod(center - block[:, 1:-1, 1:-1, :-2], block[:, 1:-1, 1:-1, 2:] - center)
    fine_cells = 2 * center.shape[1]
    child_signs = jnp.where(jnp.arange(fine_cells, dtype=jnp.int32) % 2 == 0, -1.0, 1.0).astype(
        jnp.float32
    )
    sign_z = child_signs.reshape(1, fine_cells, 1, 1)
    sign_x = child_signs.reshape(1, 1, fine_cells, 1)
    sign_y = child_signs.reshape(1, 1, 1, fine_cells)
    slopes = (
        refine_all(slope_z) * sign_z + refine_all(slope_x) * sign_x + refine_all(slope_y) * sign_y
    )
    refined = refine_all(center) + 0.25 * slopes
    return refined[:, 1:-1, 1:-1, 1:-1]


def fine_steps(fine_box, old_block, new_block):
    face_sums = None
    for substep in range(2):
        if substep == 0:
            source = old_block
        else:
            source = 0.5 * (old_block + new_block)
        padded = interpolate(source).at[:, 1:-1, 1:-1, 1:-1].set(fine_box)
        fine_box, flux_z, flux_x, flux_y = slab_advance(padded)
        boundary = jnp.stack(
            [
                flux_z[:, 0],
                flux_z[:, -1],
                flux_x[:, :, 0],
                flux_x[:, :, -1],
                flux_y[:, :, :, 0],
                flux_y[:, :, :, -1],
            ]
        )
        face_sums = boundary if face_sums is None else face_sums + boundary
    region_edge = fine_box.shape[1] // 2
    registers = 0.125 * face_sums.reshape(6, 5, region_edge, 2, region_edge, 2).sum(axis=(3, 5))
    average = 0.125 * fine_box.reshape(5, region_edge, 2, region_edge, 2, region_edge, 2).sum(
        axis=(2, 4, 6)
    )
    return (fine_box, average, registers)


def fine_steps_each(fine_boxes, old_blocks, new_blocks):

    def one_box(members):
        return fine_steps(members[0], members[1], members[2])

    return lax.map(one_box, (fine_boxes, old_blocks, new_blocks))


def block_at(field, anchor, block_edge):
    start_zero = jnp.zeros((), jnp.int32)
    return lax.dynamic_slice(
        field,
        (start_zero, anchor[0] - 2, anchor[1] - 2, anchor[2] - 2),
        (5, block_edge, block_edge, block_edge),
    )


def reflux_box(coarse_field, fluxes, anchor, registers, region_width):
    start_zero = jnp.zeros((), jnp.int32)
    for axis_pos in range(3):
        for face_side in range(2):
            face_start = [start_zero, anchor[0], anchor[1], anchor[2]]
            face_start[axis_pos + 1] = anchor[axis_pos] + face_side * region_width
            cell_start = list(face_start)
            cell_start[axis_pos + 1] = anchor[axis_pos] + (face_side * (region_width + 1) - 1)
            extent = [5, region_width, region_width, region_width]
            extent[axis_pos + 1] = 1
            coarse_face = lax.dynamic_slice(fluxes[axis_pos], face_start, extent)
            register = jnp.expand_dims(registers[2 * axis_pos + face_side], axis_pos + 1)
            outside_cells = lax.dynamic_slice(coarse_field, cell_start, extent)
            factor = RATIO * (1.0 - 2.0 * face_side)
            coarse_field = lax.dynamic_update_slice(
                coarse_field, outside_cells + factor * (coarse_face - register), cell_start
            )
    return coarse_field


def average_down(coarse_field, anchor, average):
    start_zero = jnp.zeros((), jnp.int32)
    return lax.dynamic_update_slice(
        coarse_field, average, (start_zero, anchor[0], anchor[1], anchor[2])
    )


def send_out(bundles):
    received = [bundles[0]]
    for offset in range(1, len(bundles)):
        received.append(passed_along(bundles[offset], "node", offset))
    return received


def send_back(bundles):
    received = [bundles[0]]
    for offset in range(1, len(bundles)):
        received.append(passed_along(bundles[offset], "node", -offset))
    return received


def pick_rows(received, field_pos, offsets):
    stacked = jnp.stack([bundle[field_pos] for bundle in received])
    return stacked[offsets, jnp.arange(offsets.shape[0], dtype=jnp.int32)]


def gather_field(received, field_pos):
    return jnp.concatenate([bundle[field_pos] for bundle in received])


def slot_match(cand_tags):
    count_all = cand_tags.shape[0]
    matches = cand_tags[None, :] == jnp.arange(CAP, dtype=jnp.int32)[:, None]
    live_slots = jnp.any(matches, axis=1)
    chosen = jnp.sum(jnp.where(matches, jnp.arange(count_all, dtype=jnp.int32)[None, :], 0), axis=1)
    return (live_slots, chosen)


def body(coarse_state, fine_state, fine_anchor, fine_owner):
    box_edge = coarse_state.shape[1]
    fine_edge = F
    region_edge = fine_edge // 2
    block_edge = region_edge + 4
    coarse_box = coarse_state.reshape(5, box_edge, box_edge, box_edge)
    padded = with_halo(coarse_box, (("node", 1), ("dev", 2)), 1)
    padded = jnp.concatenate([padded[..., -1:], padded, padded[..., :1]], axis=3)
    stepped, flux_z, flux_x, flux_y = slab_advance(padded)
    anchors = fine_anchor[0]
    offsets = fine_owner[0, :, 0]
    slot_tags = fine_owner[0, :, 1].astype(jnp.float32)
    old_blocks = jnp.stack(
        [block_at(coarse_box, anchors[member], block_edge) for member in range(FPC)]
    )
    new_blocks = jnp.stack(
        [block_at(stepped, anchors[member], block_edge) for member in range(FPC)]
    )
    flat_blocks = jnp.stack([old_blocks, new_blocks], axis=1).reshape(FPC, -1)
    block_bundles = [
        (
            jnp.where((offsets == offset)[:, None], flat_blocks, 0.0),
            jnp.where(offsets == offset, slot_tags, -1.0),
        )
        for offset in range(SPAN)
    ]
    arrivals = send_out(block_bundles)
    cand_blocks = gather_field(arrivals, 0)
    cand_tags = gather_field(arrivals, 1).astype(jnp.int32)
    live_slots, chosen = slot_match(cand_tags)
    slot_blocks = cand_blocks[chosen].reshape(CAP, 2, 5, block_edge, block_edge, block_edge)
    fine_boxes = fine_state.reshape(CAP, 5, fine_edge, fine_edge, fine_edge)
    new_fine, slot_average, slot_registers = fine_steps_each(
        fine_boxes, slot_blocks[:, 0], slot_blocks[:, 1]
    )
    fine_out = jnp.where(live_slots[:, None], new_fine.reshape(CAP, -1), 0.0)
    valid_rows = cand_tags >= 0
    source_rows = jnp.maximum(cand_tags, 0)
    return_average = jnp.where(valid_rows[:, None], slot_average.reshape(CAP, -1)[source_rows], 0.0)
    return_registers = jnp.where(
        valid_rows[:, None], slot_registers.reshape(CAP, -1)[source_rows], 0.0
    )
    back_bundles = [
        (
            return_average[offset * FPC : (offset + 1) * FPC],
            return_registers[offset * FPC : (offset + 1) * FPC],
        )
        for offset in range(SPAN)
    ]
    returned = send_back(back_bundles)
    averages = pick_rows(returned, 0, offsets).reshape(
        FPC, 5, region_edge, region_edge, region_edge
    )
    registers = pick_rows(returned, 1, offsets).reshape(FPC, 6, 5, region_edge, region_edge)
    coarse_out = stepped
    for member in range(FPC):
        coarse_out = reflux_box(
            coarse_out, (flux_z, flux_x, flux_y), anchors[member], registers[member], region_edge
        )
    for member in range(FPC):
        coarse_out = average_down(coarse_out, anchors[member], averages[member])
    return (
        coarse_out.reshape(5, box_edge, box_edge * box_edge),
        fine_out.reshape(CAP, 5, fine_edge * fine_edge * fine_edge),
    )


def solution(mesh):
    placed = (
        P(None, "node", "dev"),
        P(("node", "dev"), None, None),
        P(("node", "dev"), None, None),
        P(("node", "dev"), None, None),
    )
    return jax.shard_map(
        body,
        mesh=mesh,
        in_specs=placed,
        out_specs=(P(None, "node", "dev"), P(("node", "dev"), None, None)),
        check_vma=False,
    )
```

profile of v0, /device:TPU:1, one launch (start us, length us, event | category | flops | bytes accessed | tf_op | source)
XLA Modules:
  0.0 680.1 jit_solution(11097817599859807899)
XLA Ops:
  6.4 13.4 %collective-permute-start.1 = (f32[5,1,16,16]{3,2,1,0:T(8,128)S(1)}, f32[5,1,16,16]{3,2,1,0:T(8,128)S(1)}, u32[]{:S(2)}, u32[]{:S(2)}) collective-permute-start(f32[5,1,16,16]{3,2,1,0:T(8,128)S(1)} %get-tuple-element.824), channel_id=1, source_target_pairs={{8,0},{16,8},{24,16},{32,24},{40,32},{48,40},{56,48},{64,56},{72,6... | collective-permute-start | bytes 15368 | tf_op jit(solution)/shard_map/ppermute | solution.py:31
  80.5 13.1 %collective-permute-start.2 = (f32[5,18,1,16]{3,2,1,0:T(1,128)S(1)}, f32[5,18,1,16]{3,2,1,0:T(1,128)S(1)}, u32[]{:S(2)}, u32[]{:S(2)}) collective-permute-start(f32[5,18,1,16]{3,2,1,0:T(1,128)S(1)} %get-tuple-element.818), channel_id=1, source_target_pairs={{0,1},{1,2},{2,3},{3,4},{4,5},{5,6},{6,7},{7,0},{8,9},{9,10},{10,1... | collective-permute-start | bytes 17288 | tf_op jit(solution)/shard_map/ppermute | solution.py:30
  98.4 9.0 %collective-permute-done.3 = f32[5,18,1,16]{3,2,1,0:T(1,128)S(1)} collective-permute-done((f32[5,18,1,16]{3,2,1,0:T(1,128)S(1)}, f32[5,18,1,16]{3,2,1,0:T(1,128)S(1)}, u32[]{:S(2)}, u32[]{:S(2)}) %collective-permute-start.3) | collective-permute-done | bytes 5792 | tf_op jit(solution)/shard_map/ppermute | solution.py:31
  108.8 23.5 %while.116 = (s32[]{:T(128)}, f32[4,5,4,16,16]{4,3,2,1,0:T(8,128)}, f32[4,5,5,16,16]{4,3,2,1,0:T(8,128)S(1)}, f32[4,5,4,17,16]{4,3,2,1,0:T(8,128)S(1)}, f32[4,5,...) while((s32[]{:T(128)}, f32[4,5,4,16,16]{4,3,2,1,0:T(8,128)}, ...), condition=%wide.region_1.2_spmd, body=%wide.region_0.1_spmd.sunk | while | flops 281221 | bytes 7546471 | solution.py:95
  161.9 431.0 %while.119 = (s32[]{:T(128)}, f32[6,5,8,8,8]{1,4,3,2,0:T(8,128)}, f32[6,5,4,4,4]{1,4,3,2,0:T(4,128)S(1)}, f32[6,6,5,4,4]{2,4,3,1,0:T(4,128)}, f32[6,5,8,8,8]{4,2...) while((s32[]{:T(128)}, f32[6,5,8,8,8]{1,4,3,2,0:T(8,128)}, ...), condition=%wide.region_10.11_spmd, body=%wide.region_3.10_spmd.sunk | while | flops 285100 | bytes 14573695 | solution.py:173
  182.8 11.9 %scatter.12 = f32[5,10,10,10]{2,3,1,0:T(8,128)S(1)} dynamic-update-slice(f32[5,10,10,10]{2,3,1,0:T(8,128)S(1)} %get-tuple-element.1229, f32[5,8,8,8]{2,3,1,0:T(8,128)S(1)} %bitcast.374, s32[]{:T(128)} %copy.587, s32[]{:T(128)} %constant.399.clone.1..sunk.1, s32[]{:T(128)} %constant.399.clone.1..sunk.1, s32[]{:T(128)} %constant.399.clone.1..sunk.1) | dynamic-update-slice | bytes 20484 | tf_op jit(solution)/shard_map/while/body/eval_jaxpr/scatter | solution.py:147
  194.9 8.6 %while.120 = (s32[]{:T(128)}, f32[2,5,4,8,8]{3,4,2,1,0:T(8,128)S(1)}, f32[2,5,5,8,8]{3,4,2,1,0:T(8,128)S(1)}, f32[2,5,4,9,8]{3,4,2,0,1:T(8,128)S(1)}, f32[2,5,4,...) while((s32[]{:T(128)}, ...), condition=%wide.region_5.5_spmd, body=%wide.region_4.4_spmd.sunk | while | flops 72581 | bytes 4293239 | solution.py:95
  203.5 11.9 %scatter.13 = f32[5,10,10,10]{2,3,1,0:T(8,128)S(1)} dynamic-update-slice(f32[5,10,10,10]{2,3,1,0:T(8,128)S(1)} %get-tuple-element.1228, f32[5,8,8,8]{2,3,1,0:T(8,128)S(1)} %bitcast.375, s32[]{:T(128)} %copy.587, s32[]{:T(128)} %constant.399.clone.1..sunk.1, s32[]{:T(128)} %constant.399.clone.1..sunk.1, s32[]{:T(128)} %constant.399.clone.1..sunk.1) | dynamic-update-slice | bytes 20484 | tf_op jit(solution)/shard_map/while/body/eval_jaxpr/scatter | solution.py:147
  215.6 8.6 %while.121 = (s32[]{:T(128)}, f32[2,5,4,8,8]{3,4,2,1,0:T(8,128)S(1)}, f32[2,5,5,8,8]{3,4,2,1,0:T(8,128)S(1)}, f32[2,5,4,9,8]{3,4,2,0,1:T(8,128)S(1)}, f32[2,5,4,...) while((s32[]{:T(128)}, ...), condition=%wide.region_7.7_spmd, body=%wide.region_6.6_spmd.sunk | while | flops 72581 | bytes 4293239 | solution.py:95
  253.4 11.9 %scatter.12 = f32[5,10,10,10]{2,3,1,0:T(8,128)S(1)} dynamic-update-slice(f32[5,10,10,10]{2,3,1,0:T(8,128)S(1)} %get-tuple-element.1229, f32[5,8,8,8]{2,3,1,0:T(8,128)S(1)} %bitcast.374, s32[]{:T(128)} %copy.587, s32[]{:T(128)} %constant.399.clone.1..sunk.1, s32[]{:T(128)} %constant.399.clone.1..sunk.1, s32[]{:T(128)} %constant.399.clone.1..sunk.1) | dynamic-update-slice | bytes 20484 | tf_op jit(solution)/shard_map/while/body/eval_jaxpr/scatter | solution.py:147
  265.4 8.6 %while.120 = (s32[]{:T(128)}, f32[2,5,4,8,8]{3,4,2,1,0:T(8,128)S(1)}, f32[2,5,5,8,8]{3,4,2,1,0:T(8,128)S(1)}, f32[2,5,4,9,8]{3,4,2,0,1:T(8,128)S(1)}, f32[2,5,4,...) while((s32[]{:T(128)}, ...), condition=%wide.region_5.5_spmd, body=%wide.region_4.4_spmd.sunk | while | flops 72581 | bytes 4293239 | solution.py:95
  274.1 11.9 %scatter.13 = f32[5,10,10,10]{2,3,1,0:T(8,128)S(1)} dynamic-update-slice(f32[5,10,10,10]{2,3,1,0:T(8,128)S(1)} %get-tuple-element.1228, f32[5,8,8,8]{2,3,1,0:T(8,128)S(1)} %bitcast.375, s32[]{:T(128)} %copy.587, s32[]{:T(128)} %constant.399.clone.1..sunk.1, s32[]{:T(128)} %constant.399.clone.1..sunk.1, s32[]{:T(128)} %constant.399.clone.1..sunk.1) | dynamic-update-slice | bytes 20484 | tf_op jit(solution)/shard_map/while/body/eval_jaxpr/scatter | solution.py:147
  324.0 11.9 %scatter.12 = f32[5,10,10,10]{2,3,1,0:T(8,128)S(1)} dynamic-update-slice(f32[5,10,10,10]{2,3,1,0:T(8,128)S(1)} %get-tuple-element.1229, f32[5,8,8,8]{2,3,1,0:T(8,128)S(1)} %bitcast.374, s32[]{:T(128)} %copy.587, s32[]{:T(128)} %constant.399.clone.1..sunk.1, s32[]{:T(128)} %constant.399.clone.1..sunk.1, s32[]{:T(128)} %constant.399.clone.1..sunk.1) | dynamic-update-slice | bytes 20484 | tf_op jit(solution)/shard_map/while/body/eval_jaxpr/scatter | solution.py:147
  336.0 8.6 %while.120 = (s32[]{:T(128)}, f32[2,5,4,8,8]{3,4,2,1,0:T(8,128)S(1)}, f32[2,5,5,8,8]{3,4,2,1,0:T(8,128)S(1)}, f32[2,5,4,9,8]{3,4,2,0,1:T(8,128)S(1)}, f32[2,5,4,...) while((s32[]{:T(128)}, ...), condition=%wide.region_5.5_spmd, body=%wide.region_4.4_spmd.sunk | while | flops 72581 | bytes 4293239 | solution.py:95
  344.7 11.9 %scatter.13 = f32[5,10,10,10]{2,3,1,0:T(8,128)S(1)} dynamic-update-slice(f32[5,10,10,10]{2,3,1,0:T(8,128)S(1)} %get-tuple-element.1228, f32[5,8,8,8]{2,3,1,0:T(8,128)S(1)} %bitcast.375, s32[]{:T(128)} %copy.587, s32[]{:T(128)} %constant.399.clone.1..sunk.1, s32[]{:T(128)} %constant.399.clone.1..sunk.1, s32[]{:T(128)} %constant.399.clone.1..sunk.1) | dynamic-update-slice | bytes 20484 | tf_op jit(solution)/shard_map/while/body/eval_jaxpr/scatter | solution.py:147
  394.6 11.9 %scatter.12 = f32[5,10,10,10]{2,3,1,0:T(8,128)S(1)} dynamic-update-slice(f32[5,10,10,10]{2,3,1,0:T(8,128)S(1)} %get-tuple-element.1229, f32[5,8,8,8]{2,3,1,0:T(8,128)S(1)} %bitcast.374, s32[]{:T(128)} %copy.587, s32[]{:T(128)} %constant.399.clone.1..sunk.1, s32[]{:T(128)} %constant.399.clone.1..sunk.1, s32[]{:T(128)} %constant.399.clone.1..sunk.1) | dynamic-update-slice | bytes 20484 | tf_op jit(solution)/shard_map/while/body/eval_jaxpr/scatter | solution.py:147
  406.6 8.6 %while.120 = (s32[]{:T(128)}, f32[2,5,4,8,8]{3,4,2,1,0:T(8,128)S(1)}, f32[2,5,5,8,8]{3,4,2,1,0:T(8,128)S(1)}, f32[2,5,4,9,8]{3,4,2,0,1:T(8,128)S(1)}, f32[2,5,4,...) while((s32[]{:T(128)}, ...), condition=%wide.region_5.5_spmd, body=%wide.region_4.4_spmd.sunk | while | flops 72581 | bytes 4293239 | solution.py:95
  415.2 11.9 %scatter.13 = f32[5,10,10,10]{2,3,1,0:T(8,128)S(1)} dynamic-update-slice(f32[5,10,10,10]{2,3,1,0:T(8,128)S(1)} %get-tuple-element.1228, f32[5,8,8,8]{2,3,1,0:T(8,128)S(1)} %bitcast.375, s32[]{:T(128)} %copy.587, s32[]{:T(128)} %constant.399.clone.1..sunk.1, s32[]{:T(128)} %constant.399.clone.1..sunk.1, s32[]{:T(128)} %constant.399.clone.1..sunk.1) | dynamic-update-slice | bytes 20484 | tf_op jit(solution)/shard_map/while/body/eval_jaxpr/scatter | solution.py:147
  465.1 11.9 %scatter.12 = f32[5,10,10,10]{2,3,1,0:T(8,128)S(1)} dynamic-update-slice(f32[5,10,10,10]{2,3,1,0:T(8,128)S(1)} %get-tuple-element.1229, f32[5,8,8,8]{2,3,1,0:T(8,128)S(1)} %bitcast.374, s32[]{:T(128)} %copy.587, s32[]{:T(128)} %constant.399.clone.1..sunk.1, s32[]{:T(128)} %constant.399.clone.1..sunk.1, s32[]{:T(128)} %constant.399.clone.1..sunk.1) | dynamic-update-slice | bytes 20484 | tf_op jit(solution)/shard_map/while/body/eval_jaxpr/scatter | solution.py:147
  477.2 8.6 %while.120 = (s32[]{:T(128)}, f32[2,5,4,8,8]{3,4,2,1,0:T(8,128)S(1)}, f32[2,5,5,8,8]{3,4,2,1,0:T(8,128)S(1)}, f32[2,5,4,9,8]{3,4,2,0,1:T(8,128)S(1)}, f32[2,5,4,...) while((s32[]{:T(128)}, ...), condition=%wide.region_5.5_spmd, body=%wide.region_4.4_spmd.sunk | while | flops 72581 | bytes 4293239 | solution.py:95
  485.8 11.9 %scatter.13 = f32[5,10,10,10]{2,3,1,0:T(8,128)S(1)} dynamic-update-slice(f32[5,10,10,10]{2,3,1,0:T(8,128)S(1)} %get-tuple-element.1228, f32[5,8,8,8]{2,3,1,0:T(8,128)S(1)} %bitcast.375, s32[]{:T(128)} %copy.587, s32[]{:T(128)} %constant.399.clone.1..sunk.1, s32[]{:T(128)} %constant.399.clone.1..sunk.1, s32[]{:T(128)} %constant.399.clone.1..sunk.1) | dynamic-update-slice | bytes 20484 | tf_op jit(solution)/shard_map/while/body/eval_jaxpr/scatter | solution.py:147
  535.7 11.9 %scatter.12 = f32[5,10,10,10]{2,3,1,0:T(8,128)S(1)} dynamic-update-slice(f32[5,10,10,10]{2,3,1,0:T(8,128)S(1)} %get-tuple-element.1229, f32[5,8,8,8]{2,3,1,0:T(8,128)S(1)} %bitcast.374, s32[]{:T(128)} %copy.587, s32[]{:T(128)} %constant.399.clone.1..sunk.1, s32[]{:T(128)} %constant.399.clone.1..sunk.1, s32[]{:T(128)} %constant.399.clone.1..sunk.1) | dynamic-update-slice | bytes 20484 | tf_op jit(solution)/shard_map/while/body/eval_jaxpr/scatter | solution.py:147
  547.8 8.6 %while.120 = (s32[]{:T(128)}, f32[2,5,4,8,8]{3,4,2,1,0:T(8,128)S(1)}, f32[2,5,5,8,8]{3,4,2,1,0:T(8,128)S(1)}, f32[2,5,4,9,8]{3,4,2,0,1:T(8,128)S(1)}, f32[2,5,4,...) while((s32[]{:T(128)}, ...), condition=%wide.region_5.5_spmd, body=%wide.region_4.4_spmd.sunk | while | flops 72581 | bytes 4293239 | solution.py:95
  556.4 11.9 %scatter.13 = f32[5,10,10,10]{2,3,1,0:T(8,128)S(1)} dynamic-update-slice(f32[5,10,10,10]{2,3,1,0:T(8,128)S(1)} %get-tuple-element.1228, f32[5,8,8,8]{2,3,1,0:T(8,128)S(1)} %bitcast.375, s32[]{:T(128)} %copy.587, s32[]{:T(128)} %constant.399.clone.1..sunk.1, s32[]{:T(128)} %constant.399.clone.1..sunk.1, s32[]{:T(128)} %constant.399.clone.1..sunk.1) | dynamic-update-slice | bytes 20484 | tf_op jit(solution)/shard_map/while/body/eval_jaxpr/scatter | solution.py:147
  (1782 shorter events, 461.0 us)
Async XLA Ops:
  0.6 68.0 %copy-start.6 = (f32[6,5,512]{2,0,1:T(8,128)S(1)}, f32[6,5,512]{2,0,1:T(8,128)}, u32[]{:S(2)}) copy-start(f32[6,5,512]{2,0,1:T(8,128)} %param.17) | copy-start | bytes 184324
  1.8 78.5 %collective-permute-start = (f32[5,1,16,16]{3,2,1,0:T(8,128)S(1)}, f32[5,1,16,16]{3,2,1,0:T(8,128)S(1)}, u32[]{:S(2)}, u32[]{:S(2)}) collective-permute-start(f32[5,1,16,16]{3,2,1,0:T(8,128)S(1)} %get-tuple-element.825), channel_id=1, source_target_pairs={{0,8},{8,16},{16,24},{24,32},{32,40},{40,48},{48,56},{56,64},{64,7... | collective-permute-start | bytes 15368 | tf_op jit(solution)/shard_map/ppermute | solution.py:30
  6.4 74.0 %collective-permute-start.1 = (f32[5,1,16,16]{3,2,1,0:T(8,128)S(1)}, f32[5,1,16,16]{3,2,1,0:T(8,128)S(1)}, u32[]{:S(2)}, u32[]{:S(2)}) collective-permute-start(f32[5,1,16,16]{3,2,1,0:T(8,128)S(1)} %get-tuple-element.824), channel_id=1, source_target_pairs={{8,0},{16,8},{24,16},{32,24},{40,32},{48,40},{56,48},{64,56},{72,6... | collective-permute-start | bytes 15368 | tf_op jit(solution)/shard_map/ppermute | solution.py:31
  21.5 57.3 %collective-permute-start.4 = (f32[2]{0:T(128)S(1)}, f32[2]{0:T(128)S(1)}, u32[]{:S(2)}, u32[]{:S(2)}) collective-permute-start(f32[2]{0:T(128)S(1)} %get-tuple-element.847), channel_id=1, source_target_pairs={{0,8},{8,16},{16,24},{24,32},{32,40},{40,48},{48,56},{56,64},{64,7... | collective-permute-start | bytes 32 | tf_op jit(solution)/shard_map/ppermute | solution.py:20
  23.4 55.4 %collective-permute-start.5 = (f32[2]{0:T(128)S(1)}, f32[2]{0:T(128)S(1)}, u32[]{:S(2)}, u32[]{:S(2)}) collective-permute-start(f32[2]{0:T(128)S(1)} %get-tuple-element.846), channel_id=1, source_target_pairs={{0,16},{8,24},{16,32},{24,40},{32,48},{40,56},{48,64},{56,72},{64,... | collective-permute-start | bytes 32 | tf_op jit(solution)/shard_map/ppermute | solution.py:20
  25.4 53.5 %collective-permute-start.6 = (f32[2]{0:T(128)S(1)}, f32[2]{0:T(128)S(1)}, u32[]{:S(2)}, u32[]{:S(2)}) collective-permute-start(f32[2]{0:T(128)S(1)} %get-tuple-element.845), channel_id=1, source_target_pairs={{0,24},{8,32},{16,40},{24,48},{32,56},{40,64},{48,72},{56,80},{64,... | collective-permute-start | bytes 32 | tf_op jit(solution)/shard_map/ppermute | solution.py:20
  80.5 17.9 %collective-permute-start.2 = (f32[5,18,1,16]{3,2,1,0:T(1,128)S(1)}, f32[5,18,1,16]{3,2,1,0:T(1,128)S(1)}, u32[]{:S(2)}, u32[]{:S(2)}) collective-permute-start(f32[5,18,1,16]{3,2,1,0:T(1,128)S(1)} %get-tuple-element.818), channel_id=1, source_target_pairs={{0,1},{1,2},{2,3},{3,4},{4,5},{5,6},{6,7},{7,0},{8,9},{9,10},{10,1... | collective-permute-start | bytes 17288 | tf_op jit(solution)/shard_map/ppermute | solution.py:30
  93.6 13.8 %collective-permute-start.3 = (f32[5,18,1,16]{3,2,1,0:T(1,128)S(1)}, f32[5,18,1,16]{3,2,1,0:T(1,128)S(1)}, u32[]{:S(2)}, u32[]{:S(2)}) collective-permute-start(f32[5,18,1,16]{3,2,1,0:T(1,128)S(1)} %get-tuple-element.819), channel_id=1, source_target_pairs={{1,0},{2,1},{3,2},{4,3},{5,4},{6,5},{7,6},{0,7},{9,8},{10,9},{11,1... | collective-permute-start | bytes 17288 | tf_op jit(solution)/shard_map/ppermute | solution.py:31
  134.8 14.2 %collective-permute-start.7 = (f32[2,5120]{1,0:T(2,128)S(1)}, f32[2,5120]{1,0:T(2,128)S(1)}, u32[]{:S(2)}, u32[]{:S(2)}) collective-permute-start(f32[2,5120]{1,0:T(2,128)S(1)} %get-tuple-element.829), channel_id=1, source_target_pairs={{0,8},{8,16},{16,24},{24,32},{32,40},{40,48},{48,56},{56,64},{64,7... | collective-permute-start | bytes 122888 | tf_op jit(solution)/shard_map/ppermute | solution.py:20
  141.7 13.5 %collective-permute-start.8 = (f32[2,5120]{1,0:T(2,128)S(1)}, f32[2,5120]{1,0:T(2,128)S(1)}, u32[]{:S(2)}, u32[]{:S(2)}) collective-permute-start(f32[2,5120]{1,0:T(2,128)S(1)} %get-tuple-element.828), channel_id=1, source_target_pairs={{0,16},{8,24},{16,32},{24,40},{32,48},{40,56},{48,64},{56,72},{64,... | collective-permute-start | bytes 122888 | tf_op jit(solution)/shard_map/ppermute | solution.py:20
  143.6 14.0 %collective-permute-start.9 = (f32[2,5120]{1,0:T(2,128)S(1)}, f32[2,5120]{1,0:T(2,128)S(1)}, u32[]{:S(2)}, u32[]{:S(2)}) collective-permute-start(f32[2,5120]{1,0:T(2,128)S(1)} %get-tuple-element.827), channel_id=1, source_target_pairs={{0,24},{8,32},{16,40},{24,48},{32,56},{40,64},{48,72},{56,80},{64,... | collective-permute-start | bytes 122888 | tf_op jit(solution)/shard_map/ppermute | solution.py:20
  161.9 432.7 %copy-start.8 = (pred[8]{0:T(512)(128)(4,1)S(1)}, pred[8]{0:T(512)(128)(4,1)}, u32[]{:S(2)}) copy-start(pred[8]{0:T(512)(128)(4,1)} %get-tuple-element.736) | copy-start | bytes 28
  592.9 23.2 %copy-start.3 = (f32[6,5,8,8,8]{1,4,3,2,0:T(8,128)S(1)}, f32[6,5,8,8,8]{1,4,3,2,0:T(8,128)}, u32[]{:S(2)}) copy-start(f32[6,5,8,8,8]{1,4,3,2,0:T(8,128)} %get-tuple-element.509) | copy-start | bytes 184324
  594.7 22.8 %collective-permute-start.13 = (f32[2,320]{1,0:T(2,128)S(1)}, f32[2,320]{1,0:T(2,128)S(1)}, u32[]{:S(2)}, u32[]{:S(2)}) collective-permute-start(f32[2,320]{1,0:T(2,128)S(1)} %get-tuple-element.837), channel_id=1, source_target_pairs={{0,1016},{8,0},{16,8},{24,16},{32,24},{40,32},{48,40},{56,48},{64,... | collective-permute-start | bytes 7688 | tf_op jit(solution)/shard_map/ppermute | solution.py:20
  598.0 24.0 %collective-permute-start.14 = (f32[2,320]{1,0:T(2,128)S(1)}, f32[2,320]{1,0:T(2,128)S(1)}, u32[]{:S(2)}, u32[]{:S(2)}) collective-permute-start(f32[2,320]{1,0:T(2,128)S(1)} %get-tuple-element.836), channel_id=1, source_target_pairs={{0,1008},{8,1016},{16,0},{24,8},{32,16},{40,24},{48,32},{56,40},{6... | collective-permute-start | bytes 7688 | tf_op jit(solution)/shard_map/ppermute | solution.py:20
  601.5 20.7 %collective-permute-start.15 = (f32[2,320]{1,0:T(2,128)S(1)}, f32[2,320]{1,0:T(2,128)S(1)}, u32[]{:S(2)}, u32[]{:S(2)}) collective-permute-start(f32[2,320]{1,0:T(2,128)S(1)} %get-tuple-element.835), channel_id=1, source_target_pairs={{0,1000},{8,1008},{16,1016},{24,0},{32,8},{40,16},{48,24},{56,32},... | collective-permute-start | bytes 7688 | tf_op jit(solution)/shard_map/ppermute | solution.py:20
  607.6 9.1 %copy-start.9 = (pred[6]{0:T(512)(128)(4,1)S(1)}, pred[6]{0:T(512)(128)(4,1)}, u32[]{:S(2)}) copy-start(pred[6]{0:T(512)(128)(4,1)} %fusion.55) | copy-start | bytes 22
  607.9 14.2 %copy-start.7 = (s32[2]{0:T(128)S(1)}, s32[2]{0:T(128)}, u32[]{:S(2)}) copy-start(s32[2]{0:T(128)} %fusion.62) | copy-start | bytes 28
  608.6 15.4 %copy-start = (f32[5,4,4,16,16]{4,3,2,1,0:T(8,128)S(1)}, f32[5,4,4,16,16]{4,3,2,1,0:T(8,128)}, u32[]{:S(2)}) copy-start(f32[5,4,4,16,16]{4,3,2,1,0:T(8,128)} %copy.303) | copy-start | bytes 245764
  608.6 15.4 %copy-start.2 = (f32[5,4,4,16,16]{4,3,2,1,0:T(8,128)S(1)}, f32[5,4,4,16,16]{4,3,2,1,0:T(8,128)}, u32[]{:S(2)}) copy-start(f32[5,4,4,16,16]{4,3,2,1,0:T(8,128)} %copy-done.1) | copy-start | bytes 245764
  608.6 15.4 %copy-start.4 = (f32[5,1,16,16]{3,2,1,0:T(8,128)S(1)}, f32[5,1,16,16]{3,2,1,0:T(8,128)}, u32[]{:S(2)}) copy-start(f32[5,1,16,16]{3,2,1,0:T(8,128)} %slice.1721) | copy-start | bytes 15364
  608.7 14.3 %collective-permute-start.10 = (f32[2,480]{1,0:T(2,128)S(1)}, f32[2,480]{1,0:T(2,128)S(1)}, u32[]{:S(2)}, u32[]{:S(2)}) collective-permute-start(f32[2,480]{1,0:T(2,128)S(1)} %get-tuple-element.833), channel_id=1, source_target_pairs={{0,1016},{8,0},{16,8},{24,16},{32,24},{40,32},{48,40},{56,48},{64,... | collective-permute-start | bytes 11528 | tf_op jit(solution)/shard_map/ppermute | solution.py:20
  612.7 10.3 %collective-permute-start.11 = (f32[2,480]{1,0:T(2,128)S(1)}, f32[2,480]{1,0:T(2,128)S(1)}, u32[]{:S(2)}, u32[]{:S(2)}) collective-permute-start(f32[2,480]{1,0:T(2,128)S(1)} %get-tuple-element.832), channel_id=1, source_target_pairs={{0,1008},{8,1016},{16,0},{24,8},{32,16},{40,24},{48,32},{56,40},{6... | collective-permute-start | bytes 11528 | tf_op jit(solution)/shard_map/ppermute | solution.py:20
  617.4 5.8 collective-permute-start.12
  (2 other events, 2.5 us)
where the time goes:
time: 692 us; the launch traced here: 680 us
  local copies, waits for them, and re-layouts  380 us (55%)
  other arithmetic  125 us (18%)
  starting transfers between devices  74.6 us (11%)
  between operations  48.5 us (7%)
  loops' own time  34.8 us (5%)
  waiting for transfers between devices  17.8 us (3%)
    scatter x12, local copies, waits for them, and re-layouts, fine_steps(): padded = interpolate(source).at[:, 1:-1, 1:-1, 1:-1].set(fine_box)  143 us
    ppermute x12, starting transfers between devices, passed_along(): return lax.ppermute(value, axis, pairs)  39.4 us
    while x416, other arithmetic  32.7 us
    dynamic_update_slice x12, local copies, waits for them, and re-layouts, reflux_box(): lax.dynamic_update_slice(coarse_field, outside_cells + factor * (coarse_f...  32.3 us
    reshape x48, local copies, waits for them, and re-layouts, refine_all(): jnp.repeat(jnp.repeat(jnp.repeat(field, 2, axis=1), 2, axis=2), 2, axis=3)  27.3 us
    reshape x96, local copies, waits for them, and re-layouts, refine_all(): jnp.repeat(field, 2, axis=1)  23.9 us
    another operation x13, loops' own time, slab_advance(): lax.map(one_slab, jnp.arange(slab_count, dtype=jnp.int32))  23.4 us
    reshape x96, local copies, waits for them, and re-layouts, refine_all(): jnp.repeat(jnp.repeat(field, 2, axis=1), 2, axis=2)  23 us
  transfers between devices with their start and end apart: 16, of which 4 were waited for; matrix products, arithmetic and copies ran while one was open for 3% of the time, Pallas kernels for 0%

commit v1 on v0

v1 whole, which is shorter than its diff:
```python
import functools

import jax
import jax.numpy as jnp
from jax import lax
from jax.experimental import pallas as pl
from jax.experimental.pallas import tpu as pltpu
from jax.sharding import PartitionSpec as P

B = 16
ROW = B * B
CAP = 6
SPAN = 4
SLOT_ROWS = 24
GAMMA = 1.4
RATIO = 0.06
VMEM = pltpu.VMEM
SMEM = pltpu.SMEM


def iota(shape, dim):
    return lax.broadcasted_iota(jnp.int32, shape, dim)


def roll(value, shift, axis):
    size = value.shape[axis]
    return pltpu.roll(value, shift % size, axis)


def take(value, index, axis):
    return jnp.take_along_axis(value, index, axis=axis, mode="promise_in_bounds")


def pack_kernel(coarse_ref, fine_ref, slots_ref, edges_ref):
    lane = iota((B, 128), 1)
    x_low = jnp.zeros((B, 128), jnp.float32)
    x_high = jnp.zeros((B, 128), jnp.float32)
    for c in range(5):
        here = (lane >= c * B) & (lane < (c + 1) * B)
        x_low = jnp.where(here, roll(coarse_ref[c, :, :128], c * B, 1), x_low)
        x_high = jnp.where(here, roll(coarse_ref[c, :, 128:], (c + 1) * B, 1), x_high)
    edges_ref[0] = x_low
    edges_ref[1] = x_high
    for slot in range(CAP):
        for c in range(5):
            for tile in range(4):
                at = slot * SLOT_ROWS + c * 4 + tile
                slots_ref[at : at + 1, :] = fine_ref[
                    c, slot : slot + 1, tile * 128 : (tile + 1) * 128
                ]
        at = slot * SLOT_ROWS + 20
        slots_ref[at : at + 4, :] = jnp.zeros((4, 128), jnp.float32)
        if slot < 5:
            slots_ref[at : at + 1, :] = coarse_ref[slot, 0:1, :128]
            slots_ref[at + 1 : at + 2, :] = coarse_ref[slot, 0:1, 128:]


def cell_terms(state):
    inverse = 1.0 / state[0]
    squares = state[1] * state[1] + state[2] * state[2] + state[3] * state[3]
    pressure = (GAMMA - 1.0) * (state[4] - 0.5 * squares * inverse)
    sound = jnp.sqrt(GAMMA * pressure * inverse)
    return inverse, pressure, sound


def face_flux(low, low_terms, up, up_terms, member):
    def side(state, terms):
        inverse, pressure, sound = terms
        velocity = state[member] * inverse
        flux = [entry * velocity for entry in state]
        flux[member] = flux[member] + pressure
        flux[4] = flux[4] + pressure * velocity
        return flux, jnp.abs(velocity) + sound

    flux_low, speed_low = side(low, low_terms)
    flux_up, speed_up = side(up, up_terms)
    half_speed = 0.5 * jnp.maximum(speed_low, speed_up)
    return [
        0.5 * (flux_low[c] + flux_up[c]) - half_speed * (up[c] - low[c]) for c in range(5)
    ]


def minmod(lower_diff, upper_diff):
    smaller = jnp.where(jnp.abs(lower_diff) < jnp.abs(upper_diff), lower_diff, upper_diff)
    return jnp.where(lower_diff * upper_diff > 0.0, smaller, 0.0)


def step_kernel(
    anchor_ref,
    owner_ref,
    coarse_ref,
    own_ref,
    one_ref,
    two_ref,
    three_ref,
    pair_ref,
    relay_ref,
    z_before_ref,
    out_ref,
    result_ref,
    half_ref,
    boxes_ref,
):
    z0 = [anchor_ref[0, j, 0] - 2 for j in range(2)]
    x0 = [anchor_ref[0, j, 1] - 2 for j in range(2)]
    y0 = [anchor_ref[0, j, 2] - 2 for j in range(2)]
    shifts = [x0[j] * B + y0[j] for j in range(2)]

    for j in range(2):
        for k, source in enumerate((own_ref, one_ref, two_ref, three_ref)):

            @pl.when(owner_ref[0, j, 0] == k)
            def _(j=j, source=source):
                boxes_ref[j] = source[owner_ref[0, j, 1]]

    odd = lax.rem(lax.axis_index("dev"), 2)
    from_relay = relay_ref[1 - odd]
    x_before = jnp.where(odd == 1, pair_ref[1], from_relay)
    x_after = jnp.where(odd == 1, from_relay, pair_ref[0])

    state = [coarse_ref[c] for c in range(5)]
    terms = cell_terms(state)
    big = (B, ROW)
    z_at, lane = iota(big, 0), iota(big, 1)
    x_at, y_at = lane >> 4, lane & (B - 1)

    def z_neighbour(c, up):
        if up:
            edge = jnp.concatenate([one_ref[c, 20:21, :], one_ref[c, 21:22, :]], axis=1)
            return jnp.where(z_at == B - 1, edge, roll(state[c], -1, 0))
        return jnp.where(z_at == 0, z_before_ref[c, B - 1 : B, :], roll(state[c], 1, 0))

    def x_neighbour(c, up):
        if up:
            edge = roll(x_after, -(c + 1) * B, 1)
            edge = jnp.concatenate([edge, edge], axis=1)
            return jnp.where(x_at == B - 1, edge, roll(state[c], -B, 1))
        edge = roll(x_before, -c * B, 1)
        edge = jnp.concatenate([edge, edge], axis=1)
        return jnp.where(x_at == 0, edge, roll(state[c], B, 1))

    def y_neighbour(c, up):
        if up:
            return jnp.where(y_at == B - 1, roll(state[c], B - 1, 1), roll(state[c], -1, 1))
        return jnp.where(y_at == 0, roll(state[c], 1 - B, 1), roll(state[c], 1, 1))

    def offsets_in(j):
        return z_at - z0[j], x_at - x0[j], y_at - y0[j]

    def inside(offset):
        return (offset >= 2) & (offset < 6)

    change = None
    correction = [jnp.zeros(big, jnp.float32)] * 5
    for dim, (neighbour, member) in enumerate(
        ((z_neighbour, 3), (x_neighbour, 1), (y_neighbour, 2))
    ):
        low = [neighbour(c, False) for c in range(5)]
        up = [neighbour(c, True) for c in range(5)]
        flux_low = face_flux(low, cell_terms(low), state, terms, member)
        flux_high = face_flux(state, terms, up, cell_terms(up), member)
        below, above = None, None
        for j in range(2):
            off = offsets_in(j)
            others = [inside(off[other]) for other in range(3) if other != dim]
            shared = others[0] & others[1]
            is_below = shared & (off[dim] == 1)
            is_above = shared & (off[dim] == 6)
            below = is_below if below is None else below | is_below
            above = is_above if above is None else above | is_above
        difference = [flux_high[c] - flux_low[c] for c in range(5)]
        change = difference if change is None else [change[c] + difference[c] for c in range(5)]
        correction = [
            jnp.where(below, flux_high[c], jnp.where(above, -flux_low[c], correction[c]))
            for c in range(5)
        ]
    for c in range(5):
        stepped = state[c] - RATIO * change[c]
        half_ref[c] = 0.5 * (state[c] + stepped)
        out_ref[c] = stepped + RATIO * correction[c]

    small = (8, 128)
    row, lane = iota(small, 0), iota(small, 1)
    wide_row = iota((8, ROW), 0)
    half = lane < 64
    even_row = (row & 1) == 0
    box_at, b_at, e_at = lane >> 6, (lane >> 3) & 7, lane & 7
    block_x, block_box, block_y = lane >> 4, (lane >> 3) & 1, lane & 7

    def swap(value):
        return roll(value, 64, 1)

    fine = []
    for c in range(5):
        pick = (c % 2) * 4 + (row >> 1)
        rows = pl.ds((c // 2) * 8, 8)
        first = take(boxes_ref[0, rows, :], pick, 0)
        second = take(boxes_ref[1, rows, :], pick, 0)
        fine.append(
            jnp.where(
                half,
                jnp.where(even_row, first, swap(first)),
                jnp.where(even_row, swap(second), second),
            )
        )

    def block(ref, c):
        parts = []
        for j in range(2):
            rows = jnp.where(wide_row >= z0[j], ref[c, :8, :], ref[c, 8:, :])
            window = jnp.where(lane >= shifts[j], rows[:, :128], rows[:, 128:])
            window = pltpu.roll(window, (8 - z0[j]) & 7, 0)
            parts.append(pltpu.roll(window, (256 - shifts[j] + 8 * j) & 127, 1))
        return jnp.where(block_box == 0, parts[0], parts[1])

    def sign(flag):
        return jnp.where(flag, 0.25, -0.25).astype(jnp.float32)

    towards_z, towards_x, towards_y = sign(row < 4), sign(block_x < 4), sign(block_y < 4)
    child_z, child_x, child_y = (
        sign((row & 1) == 1),
        sign((b_at & 1) == 1),
        sign((e_at & 1) == 1),
    )
    mid_x, mid_y = (2 + (b_at >> 1)) * B, 2 + (e_at >> 1)
    end_x, end_y = jnp.where(b_at < 4, 1, 6) * B, jnp.where(e_at < 4, 1, 6)
    lanes_z = mid_x + box_at * 8 + mid_y
    lanes_x = end_x + box_at * 8 + mid_y
    lanes_y = mid_x + box_at * 8 + end_y
    rows_end = jnp.where(row < 4, 1, 6)
    rows_mid = 2 + (row >> 1)

    def ghosts(ref):
        ghost_z, ghost_x, ghost_y = [], [], []
        for c in range(5):
            field = block(ref, c)

            def slope(axis, step):
                lower = field - roll(field, step, axis)
                return minmod(lower, roll(lower, -step, axis))

            slope_z, slope_x, slope_y = slope(0, 1), slope(1, B), slope(1, 1)
            value = take(field + towards_z * slope_z, lanes_z, 1)
            value = value + child_x * take(slope_x, lanes_z, 1) + child_y * take(slope_y, lanes_z, 1)
            ghost_z.append(take(value, rows_end, 0))
            value = take(field + towards_x * slope_x, lanes_x, 1)
            value = value + child_y * take(slope_y, lanes_x, 1)
            ghost_x.append(
                take(value, rows_mid, 0) + child_z * take(take(slope_z, lanes_x, 1), rows_mid, 0)
            )
            value = take(field + towards_y * slope_y, lanes_y, 1)
            value = value + child_x * take(slope_x, lanes_y, 1)
            ghost_y.append(
                take(value, rows_mid, 0) + child_z * take(take(slope_z, lanes_y, 1), rows_mid, 0)
            )
        return ghost_z, ghost_x, ghost_y

    directions = ((0, 1, row, 3), (1, 8, b_at, 1), (1, 1, e_at, 2))
    sums = [None, None, None]
    for ref in (coarse_ref, half_ref):
        ghost_sets = ghosts(ref)
        terms = cell_terms(fine)
        change = None
        for dim, (axis, step, at, member) in enumerate(directions):
            ghost = ghost_sets[dim]
            low = [jnp.where(at == 0, ghost[c], roll(fine[c], step, axis)) for c in range(5)]
            up = [jnp.where(at == 7, ghost[c], roll(fine[c], -step, axis)) for c in range(5)]
            flux_low = face_flux(low, cell_terms(low), fine, terms, member)
            flux_high = face_flux(fine, terms, up, cell_terms(up), member)
            difference = [flux_high[c] - flux_low[c] for c in range(5)]
            change = difference if change is None else [change[c] + difference[c] for c in range(5)]
            edge = [jnp.where(at < 4, flux_low[c], flux_high[c]) for c in range(5)]
            sums[dim] = edge if sums[dim] is None else [sums[dim][c] + edge[c] for c in range(5)]
        fine = [fine[c] - RATIO * change[c] for c in range(5)]

    back = [[], []]
    for c in range(5):
        swapped = swap(fine[c])
        pick = (row & 3) * 2
        for j, (on_even, on_odd) in enumerate(((fine[c], swapped), (swapped, fine[c]))):
            joined = jnp.where(even_row, on_even, on_odd)
            joined = jnp.where(half, joined, roll(joined, -1, 0))
            back[j].append(take(joined, pick, 0))
    for j in range(2):
        tag = (owner_ref[0, j, 0] * 8 + owner_ref[0, j, 1]).astype(jnp.float32)
        back[j].append(jnp.full(small, tag, jnp.float32))
        for pair in range(3):
            result_ref[j, pair * 8 : pair * 8 + 8, :] = jnp.where(
                row < 4, back[j][2 * pair], back[j][2 * pair + 1]
            )

    near_x, near_y = (block_x - 2) * 16, (block_y - 2) * 2
    far_x, far_y = jnp.where(block_x < 4, 0, 56), jnp.where(block_y < 4, 0, 7)
    back_z = (block_box * 64 + near_x + near_y) & 127
    back_x = (block_box * 64 + far_x + near_y) & 127
    back_y = (block_box * 64 + near_x + far_y) & 127
    back_mid = ((row - 2) * 2) & 7
    back_end = jnp.where(row < 4, 0, 7)
    factor_z = jnp.where(row < 4, -0.125 * RATIO, 0.125 * RATIO).astype(jnp.float32)
    factor_x = jnp.where(block_x < 4, -0.125 * RATIO, 0.125 * RATIO).astype(jnp.float32)
    factor_y = jnp.where(block_y < 4, -0.125 * RATIO, 0.125 * RATIO).astype(jnp.float32)
    on_x = (block_x == 1) | (block_x == 6)
    on_y = (block_y == 1) | (block_y == 6)
    on_z = (row == 1) | (row == 6)

    def add_e(value):
        return value + roll(value, -1, 1)

    def add_b(value):
        return value + roll(value, -8, 1)

    def add_a(value):
        return value + roll(value, -1, 0)

    covered, beside = [], []
    for j in range(2):
        off = offsets_in(j)
        within = [inside(offset) for offset in off]
        at_face = [(offset == 1) | (offset == 6) for offset in off]
        covered.append(within[0] & within[1] & within[2])
        beside.append(
            (at_face[0] & within[1] & within[2])
            | (within[0] & at_face[1] & within[2])
            | (within[0] & within[1] & at_face[2])
        )
    for c in range(5):
        from_z = take(add_b(add_e(sums[0][c])), back_z, 1)
        from_x = take(add_a(add_e(sums[1][c])), back_x, 1)
        from_y = take(add_a(add_b(sums[2][c])), back_y, 1)
        average = take(add_a(add_b(add_e(fine[c]))), back_z, 1)
        mixed = jnp.where(
            on_x, factor_x * from_x, jnp.where(on_y, factor_y * from_y, 0.125 * average)
        )
        placed = jnp.where(on_z, factor_z * take(from_z, back_end, 0), take(mixed, back_mid, 0))
        value = out_ref[c]
        for j in range(2):
            moved = pltpu.roll(placed, (shifts[j] + 128 - 8 * j) & 127, 1)
            moved = pltpu.roll(moved, z0[j] & 7, 0)
            moved = jnp.concatenate([moved, moved], axis=1)
            moved = jnp.concatenate([moved, moved], axis=0)
            value = jnp.where(covered[j], moved, jnp.where(beside[j], value + moved, value))
        out_ref[c] = value


def unpack_kernel(*refs):
    sources, out_ref = refs[:SPAN], refs[SPAN]
    row = iota((8, 128), 0).astype(jnp.float32)
    matches = [
        [sources[k][j, 20:21, :] == row + 8.0 * k for j in range(2)] for k in range(SPAN)
    ]
    for c in range(5):
        for tile in range(4):
            at = c * 4 + tile
            value = jnp.zeros((8, 128), jnp.float32)
            for k in range(SPAN):
                for j in range(2):
                    value = jnp.where(matches[k][j], sources[k][j, at : at + 1, :], value)
            out_ref[c, :, tile * 128 : (tile + 1) * 128] = value[:CAP]


def moved_along(value, axis, steps):
    count = lax.axis_size(axis)
    return lax.ppermute(value, axis, [(i, (i + steps) % count) for i in range(count)])


def full(space):
    return pl.BlockSpec(memory_space=space)


def body(coarse_state, fine_state, fine_anchor, fine_owner):
    def like(*shape):
        return jax.ShapeDtypeStruct(shape, jnp.float32)

    fine_by_comp = jnp.swapaxes(fine_state, 0, 1)
    slots, edges = pl.pallas_call(
        pack_kernel,
        out_shape=(like(CAP * SLOT_ROWS, 128), like(2, B, 128)),
        in_specs=[full(VMEM)] * 2,
        out_specs=[full(VMEM)] * 2,
        name="pack",
    )(coarse_state, fine_by_comp)
    slots = slots.reshape(CAP, SLOT_ROWS, 128)
    devs = lax.axis_size("dev")
    pair = lax.ppermute(edges, "dev", [(d, d ^ 1) for d in range(devs)])
    relay = lax.ppermute(pair, "dev", [(d, (d + 2 - 4 * (d % 2)) % devs) for d in range(devs)])
    fine_parts = [slots] + [moved_along(slots, "node", -k) for k in range(1, SPAN)]
    z_before = moved_along(coarse_state, "node", 1)
    coarse_out, result = pl.pallas_call(
        step_kernel,
        out_shape=(like(5, B, ROW), like(2, SLOT_ROWS, 128)),
        in_specs=[full(SMEM)] * 2 + [full(VMEM)] * 8,
        out_specs=[full(VMEM)] * 2,
        scratch_shapes=[VMEM((5, B, ROW), jnp.float32), VMEM((2, SLOT_ROWS, 128), jnp.float32)],
        name="step",
    )(fine_anchor, fine_owner, coarse_state, *fine_parts, pair, relay, z_before)
    results = [result] + [moved_along(result, "node", k) for k in range(1, SPAN)]
    fine_out = pl.pallas_call(
        unpack_kernel,
        out_shape=like(5, CAP, 512),
        in_specs=[full(VMEM)] * SPAN,
        out_specs=full(VMEM),
        name="unpack",
    )(*results)
    return coarse_out, jnp.swapaxes(fine_out, 0, 1)


def solution(mesh):
    placed = (
        P(None, "node", "dev"),
        P(("node", "dev"), None, None),
        P(("node", "dev"), None, None),
        P(("node", "dev"), None, None),
    )
    return jax.shard_map(
        body,
        mesh=mesh,
        in_specs=placed,
        out_specs=(P(None, "node", "dev"), P(("node", "dev"), None, None)),
        check_vma=False,
    )
```

time: 692 us -> 81.5 us (0.12); the launches traced: 680 us -> 81 us
  local copies, waits for them, and re-layouts: 380 us -> 2.46 us
  other arithmetic: 125 us -> 0 us
  between operations: 48.5 us -> 0.76 us
  loops' own time: 34.8 us -> 0 us
  starting transfers between devices: 74.6 us -> 54 us
    scatter x12 -> x0, local copies, waits for them, and re-layouts: 143 us -> none  [fine_steps(): padded = interpolate(source).at[:, 1:-1, 1:-1, 1:-1].set(fine_box)]
    reshape x248 -> x0, local copies, waits for them, and re-layouts: 80.3 us -> none  [the longest x48 27.3 us: refine_all(): jnp.repeat(jnp.repeat(jnp.repeat(field, 2, axis=1), 2, axis=2), 2, axis=3)]
    dynamic_update_slice x68 -> x0, local copies, waits for them, and re-layouts: 53.8 us -> none  [the longest x12 32.3 us: reflux_box(): lax.dynamic_update_slice(coarse_field, outside_cells + factor * (coarse_f...]
    another operation x14 -> x0, loops' own time: 34.8 us -> none  [the longest x13 23.4 us: slab_advance(): lax.map(one_slab, jnp.arange(slab_count, dtype=jnp.int32))]
    while x416 -> x0, other arithmetic: 32.7 us -> none
    slice x135 -> x0, local copies, waits for them, and re-layouts: 32 us -> none  [the longest x24 7.19 us: fine_steps(): flux_y[:, :, :, -1]]
    dynamic_slice x40 -> x0, local copies, waits for them, and re-layouts: 24.6 us -> none  [the longest x28 18.4 us: slab_advance(): lax.map(one_slab, jnp.arange(slab_count, dtype=jnp.int32))]
    add x18 -> x0, other arithmetic: 21.9 us -> none  [the longest x6 13.3 us: interpolate(): refined = refine_all(center) + 0.25 * slopes]
  transfers between devices with their start and end apart: 16 -> 9, of which waited for: 4 -> 4; matrix products, arithmetic and copies ran while one was open for 3% -> 0% of each run, Pallas kernels for 0% -> 2%
where the time goes in v1:
time: 81.5 us; the launch traced here: 81 us
  starting transfers between devices  54 us (66%)
  waiting for transfers between devices  17.6 us (22%)
  Pallas kernels  6.26 us (8%)
  local copies, waits for them, and re-layouts  2.46 us (3%)
    ppermute x7, starting transfers between devices, moved_along(): lax.ppermute(value, axis, [(i, (i + steps) % count) for i in range(count)])  43.4 us
    ppermute x7, waiting for transfers between devices, moved_along(): lax.ppermute(value, axis, [(i, (i + steps) % count) for i in range(count)])  9.1 us
    ppermute x1, starting transfers between devices, body(): pair = lax.ppermute(edges, 'dev', [(d, d ^ 1) for d in range(devs)])  8.71 us
    ppermute x1, waiting for transfers between devices, body(): pair = lax.ppermute(edges, 'dev', [(d, d ^ 1) for d in range(devs)])  4.7 us
    ppermute x1, waiting for transfers between devices, body(): lax.ppermute(pair, 'dev', [(d, (d + 2 - 4 * (d % 2)) % devs) for d in ran...  3.77 us
    pallas_call x1, Pallas kernels, body(): pl.pallas_call(step_kernel, out_shape=(like(5, B, ROW), like(2, SLOT_ROWS...  3.17 us
    unnamed x18, local copies, waits for them, and re-layouts  2.46 us
    ppermute x1, starting transfers between devices, body(): lax.ppermute(pair, 'dev', [(d, (d + 2 - 4 * (d % 2)) % devs) for d in ran...  1.91 us
  transfers between devices with their start and end apart: 9, of which 4 were waited for; matrix products, arithmetic and copies ran while one was open for 0% of the time, Pallas kernels for 2%

profile of v1, /device:TPU:1, one launch (start us, length us, event | category | flops | bytes accessed | tf_op | source)
XLA Modules:
  0.0 81.0 jit_solution(897709752109818461)
XLA Ops:
  0.6 4.6 %collective-permute-start.5 = (f32[5,16,256]{2,1,0:T(8,128)}, f32[5,16,256]{2,1,0:T(8,128)S(1)}, u32[]{:S(2)}, u32[]{:S(2)}) collective-permute-start(f32[5,16,256]{2,1,0:T(8,128)} %coarse_ref.3), channel_id=1, source_target_pairs={{0,8},{8,16},{16,24},{24,32},{32,40},{40,48},{48,56},{56,64},{64,7... | collective-permute-start | bytes 245768 | tf_op jit(solution)/shard_map/ppermute | solution.py:363
  5.2 1.6 %pack.1 = (f32[144,128]{1,0:T(8,128)}, f32[2,16,128]{2,1,0:T(8,128)}) custom-call(f32[5,16,256]{2,1,0:T(8,128)} %coarse_ref.3, f32[5,6,512]{2,1,0:T(8,128)} %bitcast.3), custom_call_target="tpu_custom_call" | custom-call | tf_op jit(solution)/shard_map/pack/pallas_call | solution.py:375
  6.9 17.7 %collective-permute-start.2 = (f32[6,24,128]{2,1,0:T(8,128)}, f32[6,24,128]{2,1,0:T(8,128)S(1)}, u32[]{:S(2)}, u32[]{:S(2)}) collective-permute-start(f32[6,24,128]{2,1,0:T(8,128)} %bitcast.5), channel_id=1, source_target_pairs={{0,1000},{8,1008},{16,1016},{24,0},{32,8},{40,16},{48,24},{56,32},... | collective-permute-start | bytes 221192 | tf_op jit(solution)/shard_map/ppermute | solution.py:363
  24.5 7.7 %collective-permute-start.1 = (f32[6,24,128]{2,1,0:T(8,128)}, f32[6,24,128]{2,1,0:T(8,128)S(1)}, u32[]{:S(2)}, u32[]{:S(2)}) collective-permute-start(f32[6,24,128]{2,1,0:T(8,128)} %bitcast.6), channel_id=1, source_target_pairs={{0,1008},{8,1016},{16,0},{24,8},{32,16},{40,24},{48,32},{56,40},{6... | collective-permute-start | bytes 221192 | tf_op jit(solution)/shard_map/ppermute | solution.py:363
  32.2 1.9 %collective-permute-start = (f32[6,24,128]{2,1,0:T(8,128)}, f32[6,24,128]{2,1,0:T(8,128)S(1)}, u32[]{:S(2)}, u32[]{:S(2)}) collective-permute-start(f32[6,24,128]{2,1,0:T(8,128)} %bitcast.7), channel_id=1, source_target_pairs={{0,1016},{8,0},{16,8},{24,16},{32,24},{40,32},{48,40},{56,48},{64,... | collective-permute-start | bytes 221192 | tf_op jit(solution)/shard_map/ppermute | solution.py:363
  34.1 8.7 %collective-permute-start.3 = (f32[2,16,128]{2,1,0:T(8,128)}, f32[2,16,128]{2,1,0:T(8,128)S(1)}, u32[]{:S(2)}, u32[]{:S(2)}) collective-permute-start(f32[2,16,128]{2,1,0:T(8,128)} %get-tuple-element.7), channel_id=1, source_target_pairs={{0,1},{1,0},{2,3},{3,2},{4,5},{5,4},{6,7},{7,6},{8,9},{9,8},{10,11... | collective-permute-start | bytes 49160 | tf_op jit(solution)/shard_map/ppermute | solution.py:384
  42.9 4.7 %collective-permute-done.3.pair_ref = f32[2,16,128]{2,1,0:T(8,128)S(1)} collective-permute-done((f32[2,16,128]{2,1,0:T(8,128)}, f32[2,16,128]{2,1,0:T(8,128)S(1)}, u32[]{:S(2)}, u32[]{:S(2)}) %collective-permute-start.3) | collective-permute-done | bytes 16416 | tf_op jit(solution)/shard_map/ppermute | solution.py:384
  47.6 1.9 %collective-permute-start.4 = (f32[2,16,128]{2,1,0:T(8,128)S(1)}, f32[2,16,128]{2,1,0:T(8,128)S(1)}, u32[]{:S(2)}, u32[]{:S(2)}) collective-permute-start(f32[2,16,128]{2,1,0:T(8,128)S(1)} %collective-permute-done.3.pair_ref), channel_id=1, source_target_pairs={{0,2},{1,7},{2,4},{3,1},{4,6},{5,3},{6,0},{7,5},{8,10},{9,15},{10,... | collective-permute-start | bytes 49160 | tf_op jit(solution)/shard_map/ppermute | solution.py:385
  49.5 3.8 %collective-permute-done.4.relay_ref = f32[2,16,128]{2,1,0:T(8,128)S(1)} collective-permute-done((f32[2,16,128]{2,1,0:T(8,128)S(1)}, f32[2,16,128]{2,1,0:T(8,128)S(1)}, u32[]{:S(2)}, u32[]{:S(2)}) %collective-permute-start.4) | collective-permute-done | bytes 16416 | tf_op jit(solution)/shard_map/ppermute | solution.py:385
  53.3 0.0 collective-permute-done.one_ref
  53.3 0.5 copy-done.8
  53.9 0.0 copy-done.1
  53.9 0.0 copy-done.2
  53.9 0.0 copy-done.3
  53.9 0.6 copy-done
  54.6 3.2 %step.1 = (f32[5,16,256]{2,1,0:T(8,128)}, f32[2,24,128]{2,1,0:T(8,128)}) custom-call(s32[1,2,3]{2,1,0:T(2,128)} %anchor_ref.1, s32[1,2,2]{2,1,0:T(2,128)} %owner_ref.1, f32[5,16,256]{2,1,0:T(8,128)} %coarse_ref.3, f32[6,24,128]{2,1,0:T(8,128)} %bitcast.8, f32[6,24,128]{2,1,0:T(8,128)} %copy-done.3, f32[6,24,128]{2,1,0:T(8,128)} %copy-done.2, ...), custom_call_target="tpu_custom_call" | custom-call | tf_op jit(solution)/shard_map/step/pallas_call | solution.py:388
  57.7 7.1 %collective-permute-start.8 = (f32[2,24,128]{2,1,0:T(8,128)}, f32[2,24,128]{2,1,0:T(8,128)S(1)}, u32[]{:S(2)}, u32[]{:S(2)}) collective-permute-start(f32[2,24,128]{2,1,0:T(8,128)} %get-tuple-element.9.refs_0_), channel_id=1, source_target_pairs={{0,24},{8,32},{16,40},{24,48},{32,56},{40,64},{48,72},{56,80},{64,... | collective-permute-start | bytes 73736 | tf_op jit(solution)/shard_map/ppermute | solution.py:363
  64.8 1.9 %collective-permute-start.7 = (f32[2,24,128]{2,1,0:T(8,128)}, f32[2,24,128]{2,1,0:T(8,128)S(1)}, u32[]{:S(2)}, u32[]{:S(2)}) collective-permute-start(f32[2,24,128]{2,1,0:T(8,128)} %get-tuple-element.9.refs_0_), channel_id=1, source_target_pairs={{0,16},{8,24},{16,32},{24,40},{32,48},{40,56},{48,64},{56,72},{64,... | collective-permute-start | bytes 73736 | tf_op jit(solution)/shard_map/ppermute | solution.py:363
  66.8 2.5 %collective-permute-start.6 = (f32[2,24,128]{2,1,0:T(8,128)}, f32[2,24,128]{2,1,0:T(8,128)S(1)}, u32[]{:S(2)}, u32[]{:S(2)}) collective-permute-start(f32[2,24,128]{2,1,0:T(8,128)} %get-tuple-element.9.refs_0_), channel_id=1, source_target_pairs={{0,8},{8,16},{16,24},{24,32},{32,40},{40,48},{48,56},{56,64},{64,7... | collective-permute-start | bytes 73736 | tf_op jit(solution)/shard_map/ppermute | solution.py:363
  69.2 2.5 %collective-permute-done.8.refs_3_ = f32[2,24,128]{2,1,0:T(8,128)S(1)} collective-permute-done((f32[2,24,128]{2,1,0:T(8,128)}, f32[2,24,128]{2,1,0:T(8,128)S(1)}, u32[]{:S(2)}, u32[]{:S(2)}) %collective-permute-start.8) | collective-permute-done | bytes 24608 | tf_op jit(solution)/shard_map/ppermute | solution.py:363
  71.8 6.5 %collective-permute-done.7.refs_2_ = f32[2,24,128]{2,1,0:T(8,128)S(1)} collective-permute-done((f32[2,24,128]{2,1,0:T(8,128)}, f32[2,24,128]{2,1,0:T(8,128)S(1)}, u32[]{:S(2)}, u32[]{:S(2)}) %collective-permute-start.7) | collective-permute-done | bytes 24608 | tf_op jit(solution)/shard_map/ppermute | solution.py:363
  78.3 0.6 copy-done.5
  78.9 0.6 copy-done.6
  79.5 1.5 %unpack.1 = f32[5,6,512]{2,1,0:T(8,128)} custom-call(f32[2,24,128]{2,1,0:T(8,128)} %get-tuple-element.9.refs_0_, f32[2,24,128]{2,1,0:T(8,128)} %copy-done.6, f32[2,24,128]{2,1,0:T(8,128)} %copy-done.5, f32[2,24,128]{2,1,0:T(8,128)} %copy-done.4), custom_call_target="tpu_custom_call" | custom-call | tf_op jit(solution)/shard_map/unpack/pallas_call | solution.py:397
  (15 shorter events, 0.0 us)
Async XLA Ops:
  0.6 52.7 %collective-permute-start.5 = (f32[5,16,256]{2,1,0:T(8,128)}, f32[5,16,256]{2,1,0:T(8,128)S(1)}, u32[]{:S(2)}, u32[]{:S(2)}) collective-permute-start(f32[5,16,256]{2,1,0:T(8,128)} %coarse_ref.3), channel_id=1, source_target_pairs={{0,8},{8,16},{16,24},{24,32},{32,40},{40,48},{48,56},{56,64},{64,7... | collective-permute-start | bytes 245768 | tf_op jit(solution)/shard_map/ppermute | solution.py:363
  6.9 46.4 %collective-permute-start.2 = (f32[6,24,128]{2,1,0:T(8,128)}, f32[6,24,128]{2,1,0:T(8,128)S(1)}, u32[]{:S(2)}, u32[]{:S(2)}) collective-permute-start(f32[6,24,128]{2,1,0:T(8,128)} %bitcast.5), channel_id=1, source_target_pairs={{0,1000},{8,1008},{16,1016},{24,0},{32,8},{40,16},{48,24},{56,32},... | collective-permute-start | bytes 221192 | tf_op jit(solution)/shard_map/ppermute | solution.py:363
  24.5 28.7 %collective-permute-start.1 = (f32[6,24,128]{2,1,0:T(8,128)}, f32[6,24,128]{2,1,0:T(8,128)S(1)}, u32[]{:S(2)}, u32[]{:S(2)}) collective-permute-start(f32[6,24,128]{2,1,0:T(8,128)} %bitcast.6), channel_id=1, source_target_pairs={{0,1008},{8,1016},{16,0},{24,8},{32,16},{40,24},{48,32},{56,40},{6... | collective-permute-start | bytes 221192 | tf_op jit(solution)/shard_map/ppermute | solution.py:363
  32.2 21.1 %collective-permute-start = (f32[6,24,128]{2,1,0:T(8,128)}, f32[6,24,128]{2,1,0:T(8,128)S(1)}, u32[]{:S(2)}, u32[]{:S(2)}) collective-permute-start(f32[6,24,128]{2,1,0:T(8,128)} %bitcast.7), channel_id=1, source_target_pairs={{0,1016},{8,0},{16,8},{24,16},{32,24},{40,32},{48,40},{56,48},{64,... | collective-permute-start | bytes 221192 | tf_op jit(solution)/shard_map/ppermute | solution.py:363
  34.1 13.4 %collective-permute-start.3 = (f32[2,16,128]{2,1,0:T(8,128)}, f32[2,16,128]{2,1,0:T(8,128)S(1)}, u32[]{:S(2)}, u32[]{:S(2)}) collective-permute-start(f32[2,16,128]{2,1,0:T(8,128)} %get-tuple-element.7), channel_id=1, source_target_pairs={{0,1},{1,0},{2,3},{3,2},{4,5},{5,4},{6,7},{7,6},{8,9},{9,8},{10,11... | collective-permute-start | bytes 49160 | tf_op jit(solution)/shard_map/ppermute | solution.py:384
  47.6 5.7 %copy-start.7 = (f32[2,16,128]{2,1,0:T(8,128)}, f32[2,16,128]{2,1,0:T(8,128)S(1)}, u32[]{:S(2)}) copy-start(f32[2,16,128]{2,1,0:T(8,128)S(1)} %collective-permute-done.3.pair_ref) | copy-start | bytes 49156
  47.6 5.7 %collective-permute-start.4 = (f32[2,16,128]{2,1,0:T(8,128)S(1)}, f32[2,16,128]{2,1,0:T(8,128)S(1)}, u32[]{:S(2)}, u32[]{:S(2)}) collective-permute-start(f32[2,16,128]{2,1,0:T(8,128)S(1)} %collective-permute-done.3.pair_ref), channel_id=1, source_target_pairs={{0,2},{1,7},{2,4},{3,1},{4,6},{5,3},{6,0},{7,5},{8,10},{9,15},{10,... | collective-permute-start | bytes 49160 | tf_op jit(solution)/shard_map/ppermute | solution.py:385
  53.2 0.6 copy-start.8
  53.3 0.6 copy-start.1
  53.3 0.7 copy-start.2
  53.3 0.6 copy-start.3
  53.9 0.6 copy-start
  57.7 14.1 %collective-permute-start.8 = (f32[2,24,128]{2,1,0:T(8,128)}, f32[2,24,128]{2,1,0:T(8,128)S(1)}, u32[]{:S(2)}, u32[]{:S(2)}) collective-permute-start(f32[2,24,128]{2,1,0:T(8,128)} %get-tuple-element.9.refs_0_), channel_id=1, source_target_pairs={{0,24},{8,32},{16,40},{24,48},{32,56},{40,64},{48,72},{56,80},{64,... | collective-permute-start | bytes 73736 | tf_op jit(solution)/shard_map/ppermute | solution.py:363
  64.8 13.5 %collective-permute-start.7 = (f32[2,24,128]{2,1,0:T(8,128)}, f32[2,24,128]{2,1,0:T(8,128)S(1)}, u32[]{:S(2)}, u32[]{:S(2)}) collective-permute-start(f32[2,24,128]{2,1,0:T(8,128)} %get-tuple-element.9.refs_0_), channel_id=1, source_target_pairs={{0,16},{8,24},{16,32},{24,40},{32,48},{40,56},{48,64},{56,72},{64,... | collective-permute-start | bytes 73736 | tf_op jit(solution)/shard_map/ppermute | solution.py:363
  66.8 11.6 %collective-permute-start.6 = (f32[2,24,128]{2,1,0:T(8,128)}, f32[2,24,128]{2,1,0:T(8,128)S(1)}, u32[]{:S(2)}, u32[]{:S(2)}) collective-permute-start(f32[2,24,128]{2,1,0:T(8,128)} %get-tuple-element.9.refs_0_), channel_id=1, source_target_pairs={{0,8},{8,16},{16,24},{24,32},{32,40},{40,48},{48,56},{56,64},{64,7... | collective-permute-start | bytes 73736 | tf_op jit(solution)/shard_map/ppermute | solution.py:363
  71.8 6.5 %copy-start.4 = (f32[2,24,128]{2,1,0:T(8,128)}, f32[2,24,128]{2,1,0:T(8,128)S(1)}, u32[]{:S(2)}) copy-start(f32[2,24,128]{2,1,0:T(8,128)S(1)} %collective-permute-done.8.refs_3_) | copy-start | bytes 73732
  78.3 0.6 copy-start.5
  78.9 0.6 copy-start.6

commit v2 on v1

--- a/solution.py
+++ b/solution.py
@@ -31,7 +31,7 @@
     return jnp.take_along_axis(value, index, axis=axis, mode="promise_in_bounds")
 
 
-def pack_kernel(coarse_ref, fine_ref, slots_ref, edges_ref):
+def pack_kernel(coarse_ref, fine_ref, slots_ref, later_ref, edges_ref, z_high_ref):
     lane = iota((B, 128), 1)
     x_low = jnp.zeros((B, 128), jnp.float32)
     x_high = jnp.zeros((B, 128), jnp.float32)
@@ -39,6 +39,7 @@
         here = (lane >= c * B) & (lane < (c + 1) * B)
         x_low = jnp.where(here, roll(coarse_ref[c, :, :128], c * B, 1), x_low)
         x_high = jnp.where(here, roll(coarse_ref[c, :, 128:], (c + 1) * B, 1), x_high)
+        z_high_ref[c : c + 1, :] = coarse_ref[c, B - 1 : B, :]
     edges_ref[0] = x_low
     edges_ref[1] = x_high
     for slot in range(CAP):
@@ -53,6 +54,11 @@
         if slot < 5:
             slots_ref[at : at + 1, :] = coarse_ref[slot, 0:1, :128]
             slots_ref[at + 1 : at + 2, :] = coarse_ref[slot, 0:1, 128:]
+    later_ref[...] = slots_ref[...]
+
+
+def order_kernel(*refs):
+    del refs
 
 
 def cell_terms(state):
@@ -128,7 +134,7 @@
         if up:
             edge = jnp.concatenate([one_ref[c, 20:21, :], one_ref[c, 21:22, :]], axis=1)
             return jnp.where(z_at == B - 1, edge, roll(state[c], -1, 0))
-        return jnp.where(z_at == 0, z_before_ref[c, B - 1 : B, :], roll(state[c], 1, 0))
+        return jnp.where(z_at == 0, z_before_ref[c : c + 1, :], roll(state[c], 1, 0))
 
     def x_neighbour(c, up):
         if up:
@@ -367,24 +373,46 @@
     return pl.BlockSpec(memory_space=space)
 
 
+def in_order(*values):
+    return pl.pallas_call(
+        order_kernel,
+        out_shape=tuple(jax.ShapeDtypeStruct(value.shape, value.dtype) for value in values),
+        in_specs=[full(pl.ANY)] * len(values),
+        out_specs=tuple([full(pl.ANY)] * len(values)),
+        input_output_aliases={i: i for i in range(len(values))},
+        cost_estimate=pl.CostEstimate(flops=10**9, bytes_accessed=10**9, transcendentals=0),
+        name="order",
+    )(*values)
+
+
 def body(coarse_state, fine_state, fine_anchor, fine_owner):
     def like(*shape):
         return jax.ShapeDtypeStruct(shape, jnp.float32)
 
     fine_by_comp = jnp.swapaxes(fine_state, 0, 1)
-    slots, edges = pl.pallas_call(
+    slots, later, edges, z_high = pl.pallas_call(
         pack_kernel,
-        out_shape=(like(CAP * SLOT_ROWS, 128), like(2, B, 128)),
+        out_shape=(
+            like(CAP * SLOT_ROWS, 128),
+            like(CAP * SLOT_ROWS, 128),
+            like(2, B, 128),
+            like(5, ROW),
+        ),
         in_specs=[full(VMEM)] * 2,
-        out_specs=[full(VMEM)] * 2,
+        out_specs=[full(VMEM)] * 4,
         name="pack",
     )(coarse_state, fine_by_comp)
     slots = slots.reshape(CAP, SLOT_ROWS, 128)
     devs = lax.axis_size("dev")
     pair = lax.ppermute(edges, "dev", [(d, d ^ 1) for d in range(devs)])
+    z_before = moved_along(z_high, "node", 1)
+    third = moved_along(slots, "node", -3)
+    second = moved_along(slots, "node", -2)
+    later, pair, z_before = in_order(later, pair, z_before)
+    later = later.reshape(CAP, SLOT_ROWS, 128)
     relay = lax.ppermute(pair, "dev", [(d, (d + 2 - 4 * (d % 2)) % devs) for d in range(devs)])
-    fine_parts = [slots] + [moved_along(slots, "node", -k) for k in range(1, SPAN)]
-    z_before = moved_along(coarse_state, "node", 1)
+    relay, second, third = in_order(relay, second, third)
+    fine_parts = [slots, moved_along(later, "node", -1), second, third]
     coarse_out, result = pl.pallas_call(
         step_kernel,
         out_shape=(like(5, B, ROW), like(2, SLOT_ROWS, 128)),

time: 81.5 us -> 73.5 us (0.902)
  waiting for transfers between devices: 17.6 us -> 10.3 us
  starting transfers between devices: 54 us -> 51.6 us
  local copies, waits for them, and re-layouts: 2.46 us -> 3.68 us
    ppermute x7, starting transfers between devices: 43.4 us -> 28.6 us  [moved_along(): lax.ppermute(value, axis, [(i, (i + steps) % count) for i in range(count)])]
    ppermute x1, starting transfers between devices: 8.71 us -> 19.9 us  [body(): pair = lax.ppermute(edges, 'dev', [(d, d ^ 1) for d in range(devs)])]
    ppermute x1, waiting for transfers between devices: 4.7 us -> 0.01 us  [body(): pair = lax.ppermute(edges, 'dev', [(d, d ^ 1) for d in range(devs)])]
    ppermute x1, waiting for transfers between devices: 3.77 us -> 0.01 us  [body(): lax.ppermute(pair, 'dev', [(d, (d + 2 - 4 * (d % 2)) % devs) for d in ran...]
    unnamed x18, local copies, waits for them, and re-layouts: 2.46 us -> 3.68 us
    ppermute x7, waiting for transfers between devices: 9.1 us -> 10.3 us  [moved_along(): lax.ppermute(value, axis, [(i, (i + steps) % count) for i in range(count)])]
    ppermute x1, starting transfers between devices: 1.91 us -> 3.11 us  [body(): lax.ppermute(pair, 'dev', [(d, (d + 2 - 4 * (d % 2)) % devs) for d in ran...]
    pallas_call x1 -> x3, Pallas kernels: 1.62 us -> 1.64 us  [the longest x1 1.64 us: body(): pl.pallas_call(pack_kernel, out_shape=(like(CAP * SLOT_ROWS, 128), like(C...]
  transfers between devices with their start and end apart: 9 -> 9, of which waited for: 4 -> 3; matrix products, arithmetic and copies ran while one was open for 0% -> 0% of each run, Pallas kernels for 2% -> 0%
where the time goes in v2:
time: 73.5 us; the launch traced here: 72.7 us
  starting transfers between devices  51.6 us (70%)
  waiting for transfers between devices  10.3 us (14%)
  Pallas kernels  6.23 us (8%)
  local copies, waits for them, and re-layouts  3.68 us (5%)
  between operations  0.79 us (1%)
    ppermute x7, starting transfers between devices, moved_along(): lax.ppermute(value, axis, [(i, (i + steps) % count) for i in range(count)])  28.6 us
    ppermute x1, starting transfers between devices, body(): pair = lax.ppermute(edges, 'dev', [(d, d ^ 1) for d in range(devs)])  19.9 us
    ppermute x7, waiting for transfers between devices, moved_along(): lax.ppermute(value, axis, [(i, (i + steps) % count) for i in range(count)])  10.3 us
    unnamed x18, local copies, waits for them, and re-layouts  3.68 us
    pallas_call x1, Pallas kernels, body(): pl.pallas_call(step_kernel, out_shape=(like(5, B, ROW), like(2, SLOT_ROWS...  3.12 us
    ppermute x1, starting transfers between devices, body(): lax.ppermute(pair, 'dev', [(d, (d + 2 - 4 * (d % 2)) % devs) for d in ran...  3.11 us
    pallas_call x1, Pallas kernels, body(): pl.pallas_call(pack_kernel, out_shape=(like(CAP * SLOT_ROWS, 128), like(C...  1.64 us
  transfers between devices with their start and end apart: 9, of which 3 were waited for; matrix products, arithmetic and copies ran while one was open for 0% of the time, Pallas kernels for 0%

profile of v2, /device:TPU:1, one launch (start us, length us, event | category | flops | bytes accessed | tf_op | source)
XLA Modules:
  0.0 72.7 jit_solution(1831907810560553472)
XLA Ops:
  0.6 1.6 %pack.1 = (f32[144,128]{1,0:T(8,128)}, f32[144,128]{1,0:T(8,128)}, f32[2,16,128]{2,1,0:T(8,128)}, f32[5,256]{1,0:T(8,128)}) custom-call(f32[5,16,256]{2,1,0:T(8,128)} %coarse_ref.3, f32[5,6,512]{2,1,0:T(8,128)} %bitcast.4), custom_call_target="tpu_custom_call" | custom-call | tf_op jit(solution)/shard_map/pack/pallas_call | solution.py:393
  2.3 19.9 %collective-permute-start = (f32[2,16,128]{2,1,0:T(8,128)}, f32[2,16,128]{2,1,0:T(8,128)S(1)}, u32[]{:S(2)}, u32[]{:S(2)}) collective-permute-start(f32[2,16,128]{2,1,0:T(8,128)} %get-tuple-element.16), channel_id=1, source_target_pairs={{0,1},{1,0},{2,3},{3,2},{4,5},{5,4},{6,7},{7,6},{8,9},{9,8},{10,11... | collective-permute-start | bytes 49160 | tf_op jit(solution)/shard_map/ppermute | solution.py:407
  22.2 4.0 %collective-permute-start.1 = (f32[5,256]{1,0:T(8,128)}, f32[5,256]{1,0:T(8,128)S(1)}, u32[]{:S(2)}, u32[]{:S(2)}) collective-permute-start(f32[5,256]{1,0:T(8,128)} %get-tuple-element.17), channel_id=1, source_target_pairs={{0,8},{8,16},{16,24},{24,32},{32,40},{40,48},{48,56},{56,64},{64,7... | collective-permute-start | bytes 15368 | tf_op jit(solution)/shard_map/ppermute | solution.py:369
  26.2 10.2 %collective-permute-start.5 = (f32[6,24,128]{2,1,0:T(8,128)}, f32[6,24,128]{2,1,0:T(8,128)S(1)}, u32[]{:S(2)}, u32[]{:S(2)}) collective-permute-start(f32[6,24,128]{2,1,0:T(8,128)} %bitcast.6), channel_id=1, source_target_pairs={{0,1000},{8,1008},{16,1016},{24,0},{32,8},{40,16},{48,24},{56,32},... | collective-permute-start | bytes 221192 | tf_op jit(solution)/shard_map/ppermute | solution.py:369
  36.4 3.0 %collective-permute-start.4 = (f32[6,24,128]{2,1,0:T(8,128)}, f32[6,24,128]{2,1,0:T(8,128)S(1)}, u32[]{:S(2)}, u32[]{:S(2)}) collective-permute-start(f32[6,24,128]{2,1,0:T(8,128)} %bitcast.7), channel_id=1, source_target_pairs={{0,1008},{8,1016},{16,0},{24,8},{32,16},{40,24},{48,32},{56,40},{6... | collective-permute-start | bytes 221192 | tf_op jit(solution)/shard_map/ppermute | solution.py:369
  39.4 0.0 collective-permute-done.1.refs_2_
  39.4 0.6 copy-done.8
  40.0 0.0 copy-done.6
  40.0 3.1 %collective-permute-start.3 = (f32[2,16,128]{2,1,0:T(8,128)}, f32[2,16,128]{2,1,0:T(8,128)S(1)}, u32[]{:S(2)}, u32[]{:S(2)}) collective-permute-start(f32[2,16,128]{2,1,0:T(8,128)} %get-tuple-element.19.pair_ref), channel_id=1, source_target_pairs={{0,2},{1,7},{2,4},{3,1},{4,6},{5,3},{6,0},{7,5},{8,10},{9,15},{10,... | collective-permute-start | bytes 49160 | tf_op jit(solution)/shard_map/ppermute | solution.py:413
  43.1 4.0 %collective-permute-start.2 = (f32[6,24,128]{2,1,0:T(8,128)}, f32[6,24,128]{2,1,0:T(8,128)S(1)}, u32[]{:S(2)}, u32[]{:S(2)}) collective-permute-start(f32[6,24,128]{2,1,0:T(8,128)} %bitcast.9), channel_id=1, source_target_pairs={{0,1016},{8,0},{16,8},{24,16},{32,24},{40,32},{48,40},{56,48},{64,... | collective-permute-start | bytes 221192 | tf_op jit(solution)/shard_map/ppermute | solution.py:369
  47.2 0.6 copy-done.7
  47.8 0.1 copy-done
  47.9 0.6 copy-done.1
  48.5 1.2 %collective-permute-done.2.one_ref = f32[6,24,128]{2,1,0:T(8,128)S(1)} collective-permute-done((f32[6,24,128]{2,1,0:T(8,128)}, f32[6,24,128]{2,1,0:T(8,128)S(1)}, u32[]{:S(2)}, u32[]{:S(2)}) %collective-permute-start.2) | collective-permute-done | bytes 73760 | tf_op jit(solution)/shard_map/ppermute | solution.py:369
  49.7 0.6 copy-done.2
  50.3 3.1 %step.1 = (f32[5,16,256]{2,1,0:T(8,128)}, f32[2,24,128]{2,1,0:T(8,128)}) custom-call(s32[1,2,3]{2,1,0:T(2,128)} %anchor_ref.1, s32[1,2,2]{2,1,0:T(2,128)} %owner_ref.1, f32[5,16,256]{2,1,0:T(8,128)} %coarse_ref.3, f32[6,24,128]{2,1,0:T(8,128)} %bitcast.8, f32[6,24,128]{2,1,0:T(8,128)} %copy-done.2, f32[6,24,128]{2,1,0:T(8,128)} %get-tuple-element.20.two_ref, ...), custom_call_target="tpu_custom_call" | custom-call | tf_op jit(solution)/shard_map/step/pallas_call | solution.py:416
  53.5 3.0 %collective-permute-start.8 = (f32[2,24,128]{2,1,0:T(8,128)}, f32[2,24,128]{2,1,0:T(8,128)S(1)}, u32[]{:S(2)}, u32[]{:S(2)}) collective-permute-start(f32[2,24,128]{2,1,0:T(8,128)} %get-tuple-element.25.refs_0_), channel_id=1, source_target_pairs={{0,24},{8,32},{16,40},{24,48},{32,56},{40,64},{48,72},{56,80},{64,... | collective-permute-start | bytes 73736 | tf_op jit(solution)/shard_map/ppermute | solution.py:369
  56.5 1.9 %collective-permute-start.7 = (f32[2,24,128]{2,1,0:T(8,128)}, f32[2,24,128]{2,1,0:T(8,128)S(1)}, u32[]{:S(2)}, u32[]{:S(2)}) collective-permute-start(f32[2,24,128]{2,1,0:T(8,128)} %get-tuple-element.25.refs_0_), channel_id=1, source_target_pairs={{0,16},{8,24},{16,32},{24,40},{32,48},{40,56},{48,64},{56,72},{64,... | collective-permute-start | bytes 73736 | tf_op jit(solution)/shard_map/ppermute | solution.py:369
  58.4 2.5 %collective-permute-start.6 = (f32[2,24,128]{2,1,0:T(8,128)}, f32[2,24,128]{2,1,0:T(8,128)S(1)}, u32[]{:S(2)}, u32[]{:S(2)}) collective-permute-start(f32[2,24,128]{2,1,0:T(8,128)} %get-tuple-element.25.refs_0_), channel_id=1, source_target_pairs={{0,8},{8,16},{16,24},{24,32},{32,40},{40,48},{48,56},{56,64},{64,7... | collective-permute-start | bytes 73736 | tf_op jit(solution)/shard_map/ppermute | solution.py:369
  60.9 6.8 %collective-permute-done.8.refs_3_ = f32[2,24,128]{2,1,0:T(8,128)S(1)} collective-permute-done((f32[2,24,128]{2,1,0:T(8,128)}, f32[2,24,128]{2,1,0:T(8,128)S(1)}, u32[]{:S(2)}, u32[]{:S(2)}) %collective-permute-start.8) | collective-permute-done | bytes 24608 | tf_op jit(solution)/shard_map/ppermute | solution.py:369
  67.7 2.3 %collective-permute-done.7.refs_2_ = f32[2,24,128]{2,1,0:T(8,128)S(1)} collective-permute-done((f32[2,24,128]{2,1,0:T(8,128)}, f32[2,24,128]{2,1,0:T(8,128)S(1)}, u32[]{:S(2)}, u32[]{:S(2)}) %collective-permute-start.7) | collective-permute-done | bytes 24608 | tf_op jit(solution)/shard_map/ppermute | solution.py:369
  70.0 0.6 copy-done.4
  70.6 0.6 copy-done.5
  71.2 1.5 %unpack.1 = f32[5,6,512]{2,1,0:T(8,128)} custom-call(f32[2,24,128]{2,1,0:T(8,128)} %get-tuple-element.25.refs_0_, f32[2,24,128]{2,1,0:T(8,128)} %copy-done.5, f32[2,24,128]{2,1,0:T(8,128)} %copy-done.4, f32[2,24,128]{2,1,0:T(8,128)} %copy-done.3), custom_call_target="tpu_custom_call" | custom-call | tf_op jit(solution)/shard_map/unpack/pallas_call | solution.py:425
  (17 shorter events, 0.0 us)
Async XLA Ops:
  2.3 37.2 %collective-permute-start = (f32[2,16,128]{2,1,0:T(8,128)}, f32[2,16,128]{2,1,0:T(8,128)S(1)}, u32[]{:S(2)}, u32[]{:S(2)}) collective-permute-start(f32[2,16,128]{2,1,0:T(8,128)} %get-tuple-element.16), channel_id=1, source_target_pairs={{0,1},{1,0},{2,3},{3,2},{4,5},{5,4},{6,7},{7,6},{8,9},{9,8},{10,11... | collective-permute-start | bytes 49160 | tf_op jit(solution)/shard_map/ppermute | solution.py:407
  22.2 17.2 %collective-permute-start.1 = (f32[5,256]{1,0:T(8,128)}, f32[5,256]{1,0:T(8,128)S(1)}, u32[]{:S(2)}, u32[]{:S(2)}) collective-permute-start(f32[5,256]{1,0:T(8,128)} %get-tuple-element.17), channel_id=1, source_target_pairs={{0,8},{8,16},{16,24},{24,32},{32,40},{40,48},{48,56},{56,64},{64,7... | collective-permute-start | bytes 15368 | tf_op jit(solution)/shard_map/ppermute | solution.py:369
  26.2 21.0 %collective-permute-start.5 = (f32[6,24,128]{2,1,0:T(8,128)}, f32[6,24,128]{2,1,0:T(8,128)S(1)}, u32[]{:S(2)}, u32[]{:S(2)}) collective-permute-start(f32[6,24,128]{2,1,0:T(8,128)} %bitcast.6), channel_id=1, source_target_pairs={{0,1000},{8,1008},{16,1016},{24,0},{32,8},{40,16},{48,24},{56,32},... | collective-permute-start | bytes 221192 | tf_op jit(solution)/shard_map/ppermute | solution.py:369
  36.4 10.8 %collective-permute-start.4 = (f32[6,24,128]{2,1,0:T(8,128)}, f32[6,24,128]{2,1,0:T(8,128)S(1)}, u32[]{:S(2)}, u32[]{:S(2)}) collective-permute-start(f32[6,24,128]{2,1,0:T(8,128)} %bitcast.7), channel_id=1, source_target_pairs={{0,1008},{8,1016},{16,0},{24,8},{32,16},{40,24},{48,32},{56,40},{6... | collective-permute-start | bytes 221192 | tf_op jit(solution)/shard_map/ppermute | solution.py:369
  39.4 0.6 copy-start.8
  39.4 0.6 copy-start.6
  40.0 7.2 %collective-permute-start.3 = (f32[2,16,128]{2,1,0:T(8,128)}, f32[2,16,128]{2,1,0:T(8,128)S(1)}, u32[]{:S(2)}, u32[]{:S(2)}) collective-permute-start(f32[2,16,128]{2,1,0:T(8,128)} %get-tuple-element.19.pair_ref), channel_id=1, source_target_pairs={{0,2},{1,7},{2,4},{3,1},{4,6},{5,3},{6,0},{7,5},{8,10},{9,15},{10,... | collective-permute-start | bytes 49160 | tf_op jit(solution)/shard_map/ppermute | solution.py:413
  43.1 6.6 %collective-permute-start.2 = (f32[6,24,128]{2,1,0:T(8,128)}, f32[6,24,128]{2,1,0:T(8,128)S(1)}, u32[]{:S(2)}, u32[]{:S(2)}) collective-permute-start(f32[6,24,128]{2,1,0:T(8,128)} %bitcast.9), channel_id=1, source_target_pairs={{0,1016},{8,0},{16,8},{24,16},{32,24},{40,32},{48,40},{56,48},{64,... | collective-permute-start | bytes 221192 | tf_op jit(solution)/shard_map/ppermute | solution.py:369
  47.2 0.6 copy-start.7
  47.2 0.6 copy-start
  47.9 0.6 copy-start.1
  49.7 0.6 copy-start.2
  53.5 14.2 %collective-permute-start.8 = (f32[2,24,128]{2,1,0:T(8,128)}, f32[2,24,128]{2,1,0:T(8,128)S(1)}, u32[]{:S(2)}, u32[]{:S(2)}) collective-permute-start(f32[2,24,128]{2,1,0:T(8,128)} %get-tuple-element.25.refs_0_), channel_id=1, source_target_pairs={{0,24},{8,32},{16,40},{24,48},{32,56},{40,64},{48,72},{56,80},{64,... | collective-permute-start | bytes 73736 | tf_op jit(solution)/shard_map/ppermute | solution.py:369
  56.5 13.5 %collective-permute-start.7 = (f32[2,24,128]{2,1,0:T(8,128)}, f32[2,24,128]{2,1,0:T(8,128)S(1)}, u32[]{:S(2)}, u32[]{:S(2)}) collective-permute-start(f32[2,24,128]{2,1,0:T(8,128)} %get-tuple-element.25.refs_0_), channel_id=1, source_target_pairs={{0,16},{8,24},{16,32},{24,40},{32,48},{40,56},{48,64},{56,72},{64,... | collective-permute-start | bytes 73736 | tf_op jit(solution)/shard_map/ppermute | solution.py:369
  58.4 11.6 %collective-permute-start.6 = (f32[2,24,128]{2,1,0:T(8,128)}, f32[2,24,128]{2,1,0:T(8,128)S(1)}, u32[]{:S(2)}, u32[]{:S(2)}) collective-permute-start(f32[2,24,128]{2,1,0:T(8,128)} %get-tuple-element.25.refs_0_), channel_id=1, source_target_pairs={{0,8},{8,16},{16,24},{24,32},{32,40},{40,48},{48,56},{56,64},{64,7... | collective-permute-start | bytes 73736 | tf_op jit(solution)/shard_map/ppermute | solution.py:369
  67.7 2.3 %copy-start.3 = (f32[2,24,128]{2,1,0:T(8,128)}, f32[2,24,128]{2,1,0:T(8,128)S(1)}, u32[]{:S(2)}) copy-start(f32[2,24,128]{2,1,0:T(8,128)S(1)} %collective-permute-done.8.refs_3_) | copy-start | bytes 73732
  70.0 0.6 copy-start.4
  70.6 0.6 copy-start.5

commit v3 on v2

--- a/solution.py
+++ b/solution.py
@@ -102,11 +102,13 @@
     pair_ref,
     relay_ref,
     z_before_ref,
+    token_ref,
     out_ref,
     result_ref,
     half_ref,
     boxes_ref,
 ):
+    del token_ref
     z0 = [anchor_ref[0, j, 0] - 2 for j in range(2)]
     x0 = [anchor_ref[0, j, 1] - 2 for j in range(2)]
     y0 = [anchor_ref[0, j, 2] - 2 for j in range(2)]
@@ -377,8 +379,8 @@
     return pl.pallas_call(
         order_kernel,
         out_shape=tuple(jax.ShapeDtypeStruct(value.shape, value.dtype) for value in values),
-        in_specs=[full(pl.ANY)] * len(values),
-        out_specs=tuple([full(pl.ANY)] * len(values)),
+        in_specs=[full(pl.ANY)] + [full(pltpu.HBM)] * (len(values) - 1),
+        out_specs=tuple([full(pl.ANY)] + [full(pltpu.HBM)] * (len(values) - 1)),
         input_output_aliases={i: i for i in range(len(values))},
         cost_estimate=pl.CostEstimate(flops=10**9, bytes_accessed=10**9, transcendentals=0),
         name="order",
@@ -411,16 +413,23 @@
     later, pair, z_before = in_order(later, pair, z_before)
     later = later.reshape(CAP, SLOT_ROWS, 128)
     relay = lax.ppermute(pair, "dev", [(d, (d + 2 - 4 * (d % 2)) % devs) for d in range(devs)])
-    relay, second, third = in_order(relay, second, third)
+    token = pl.pallas_call(
+        order_kernel,
+        out_shape=like(8, 128),
+        in_specs=[full(pltpu.HBM)] * 3,
+        out_specs=full(pltpu.HBM),
+        cost_estimate=pl.CostEstimate(flops=10**9, bytes_accessed=10**9, transcendentals=0),
+        name="order",
+    )(relay, second, third)
     fine_parts = [slots, moved_along(later, "node", -1), second, third]
     coarse_out, result = pl.pallas_call(
         step_kernel,
         out_shape=(like(5, B, ROW), like(2, SLOT_ROWS, 128)),
-        in_specs=[full(SMEM)] * 2 + [full(VMEM)] * 8,
+        in_specs=[full(SMEM)] * 2 + [full(VMEM)] * 8 + [full(pl.ANY)],
         out_specs=[full(VMEM)] * 2,
         scratch_shapes=[VMEM((5, B, ROW), jnp.float32), VMEM((2, SLOT_ROWS, 128), jnp.float32)],
         name="step",
-    )(fine_anchor, fine_owner, coarse_state, *fine_parts, pair, relay, z_before)
+    )(fine_anchor, fine_owner, coarse_state, *fine_parts, pair, relay, z_before, token)
     results = [result] + [moved_along(result, "node", k) for k in range(1, SPAN)]
     fine_out = pl.pallas_call(
         unpack_kernel,

time: 73.5 us -> 73.4 us (level)
  no operation moved by 1% of the time
where the time goes in v3:
time: 73.4 us; the launch traced here: 72.6 us
  starting transfers between devices  51.6 us (70%)
  waiting for transfers between devices  10.3 us (14%)
  Pallas kernels  6.23 us (8%)
  local copies, waits for them, and re-layouts  3.63 us (5%)
  between operations  0.79 us (1%)
    ppermute x7, starting transfers between devices, moved_along(): lax.ppermute(value, axis, [(i, (i + steps) % count) for i in range(count)])  28.6 us
    ppermute x1, starting transfers between devices, body(): pair = lax.ppermute(edges, 'dev', [(d, d ^ 1) for d in range(devs)])  19.9 us
    ppermute x7, waiting for transfers between devices, moved_along(): lax.ppermute(value, axis, [(i, (i + steps) % count) for i in range(count)])  10.3 us
    unnamed x18, local copies, waits for them, and re-layouts  3.63 us
    pallas_call x1, Pallas kernels, body(): pl.pallas_call(step_kernel, out_shape=(like(5, B, ROW), like(2, SLOT_ROWS...  3.12 us
    ppermute x1, starting transfers between devices, body(): lax.ppermute(pair, 'dev', [(d, (d + 2 - 4 * (d % 2)) % devs) for d in ran...  3.11 us
    pallas_call x1, Pallas kernels, body(): pl.pallas_call(pack_kernel, out_shape=(like(CAP * SLOT_ROWS, 128), like(C...  1.64 us
  transfers between devices with their start and end apart: 9, of which 3 were waited for; matrix products, arithmetic and copies ran while one was open for 0% of the time, Pallas kernels for 0%

profile of v3, /device:TPU:1, one launch (start us, length us, event | category | flops | bytes accessed | tf_op | source)
XLA Modules:
  0.0 72.6 jit_solution(10651481432509612945)
XLA Ops:
  0.6 1.6 %pack.1 = (f32[144,128]{1,0:T(8,128)}, f32[144,128]{1,0:T(8,128)}, f32[2,16,128]{2,1,0:T(8,128)}, f32[5,256]{1,0:T(8,128)}) custom-call(f32[5,16,256]{2,1,0:T(8,128)} %coarse_ref.3, f32[5,6,512]{2,1,0:T(8,128)} %bitcast.4), custom_call_target="tpu_custom_call" | custom-call | tf_op jit(solution)/shard_map/pack/pallas_call | solution.py:395
  2.3 19.9 %collective-permute-start = (f32[2,16,128]{2,1,0:T(8,128)}, f32[2,16,128]{2,1,0:T(8,128)S(1)}, u32[]{:S(2)}, u32[]{:S(2)}) collective-permute-start(f32[2,16,128]{2,1,0:T(8,128)} %get-tuple-element.13), channel_id=1, source_target_pairs={{0,1},{1,0},{2,3},{3,2},{4,5},{5,4},{6,7},{7,6},{8,9},{9,8},{10,11... | collective-permute-start | bytes 49160 | tf_op jit(solution)/shard_map/ppermute | solution.py:409
  22.2 4.0 %collective-permute-start.1 = (f32[5,256]{1,0:T(8,128)}, f32[5,256]{1,0:T(8,128)S(1)}, u32[]{:S(2)}, u32[]{:S(2)}) collective-permute-start(f32[5,256]{1,0:T(8,128)} %get-tuple-element.14), channel_id=1, source_target_pairs={{0,8},{8,16},{16,24},{24,32},{32,40},{40,48},{48,56},{56,64},{64,7... | collective-permute-start | bytes 15368 | tf_op jit(solution)/shard_map/ppermute | solution.py:371
  26.2 10.2 %collective-permute-start.4 = (f32[6,24,128]{2,1,0:T(8,128)}, f32[6,24,128]{2,1,0:T(8,128)S(1)}, u32[]{:S(2)}, u32[]{:S(2)}) collective-permute-start(f32[6,24,128]{2,1,0:T(8,128)} %bitcast.6), channel_id=1, source_target_pairs={{0,1000},{8,1008},{16,1016},{24,0},{32,8},{40,16},{48,24},{56,32},... | collective-permute-start | bytes 221192 | tf_op jit(solution)/shard_map/ppermute | solution.py:371
  36.4 3.0 %collective-permute-start.3 = (f32[6,24,128]{2,1,0:T(8,128)}, f32[6,24,128]{2,1,0:T(8,128)S(1)}, u32[]{:S(2)}, u32[]{:S(2)}) collective-permute-start(f32[6,24,128]{2,1,0:T(8,128)} %bitcast.7), channel_id=1, source_target_pairs={{0,1008},{8,1016},{16,0},{24,8},{32,16},{40,24},{48,32},{56,40},{6... | collective-permute-start | bytes 221192 | tf_op jit(solution)/shard_map/ppermute | solution.py:371
  39.4 0.0 collective-permute-done.1.refs_2_
  39.4 0.5 copy-done.8
  40.0 0.0 copy-done.7
  40.0 3.1 %collective-permute-start.5 = (f32[2,16,128]{2,1,0:T(8,128)}, f32[2,16,128]{2,1,0:T(8,128)S(1)}, u32[]{:S(2)}, u32[]{:S(2)}) collective-permute-start(f32[2,16,128]{2,1,0:T(8,128)} %get-tuple-element.16.pair_ref), channel_id=1, source_target_pairs={{0,2},{1,7},{2,4},{3,1},{4,6},{5,3},{6,0},{7,5},{8,10},{9,15},{10,... | collective-permute-start | bytes 49160 | tf_op jit(solution)/shard_map/ppermute | solution.py:415
  43.1 4.0 %collective-permute-start.2 = (f32[6,24,128]{2,1,0:T(8,128)}, f32[6,24,128]{2,1,0:T(8,128)S(1)}, u32[]{:S(2)}, u32[]{:S(2)}) collective-permute-start(f32[6,24,128]{2,1,0:T(8,128)} %bitcast.9), channel_id=1, source_target_pairs={{0,1016},{8,0},{16,8},{24,16},{32,24},{40,32},{48,40},{56,48},{64,... | collective-permute-start | bytes 221192 | tf_op jit(solution)/shard_map/ppermute | solution.py:371
  47.2 0.6 copy-done.6
  47.8 0.0 copy-done
  47.8 0.6 copy-done.1
  48.5 1.2 %collective-permute-done.2.one_ref = f32[6,24,128]{2,1,0:T(8,128)S(1)} collective-permute-done((f32[6,24,128]{2,1,0:T(8,128)}, f32[6,24,128]{2,1,0:T(8,128)S(1)}, u32[]{:S(2)}, u32[]{:S(2)}) %collective-permute-start.2) | collective-permute-done | bytes 73760 | tf_op jit(solution)/shard_map/ppermute | solution.py:371
  49.7 0.6 copy-done.2
  50.3 3.1 %step.1 = (f32[5,16,256]{2,1,0:T(8,128)}, f32[2,24,128]{2,1,0:T(8,128)}) custom-call(s32[1,2,3]{2,1,0:T(2,128)} %anchor_ref.1, s32[1,2,2]{2,1,0:T(2,128)} %owner_ref.1, f32[5,16,256]{2,1,0:T(8,128)} %coarse_ref.3, f32[6,24,128]{2,1,0:T(8,128)} %bitcast.8, f32[6,24,128]{2,1,0:T(8,128)} %copy-done.2, f32[6,24,128]{2,1,0:T(8,128)} %copy-done.1, ...), custom_call_target="tpu_custom_call" | custom-call | tf_op jit(solution)/shard_map/step/pallas_call | solution.py:425
  53.4 3.0 %collective-permute-start.8 = (f32[2,24,128]{2,1,0:T(8,128)}, f32[2,24,128]{2,1,0:T(8,128)S(1)}, u32[]{:S(2)}, u32[]{:S(2)}) collective-permute-start(f32[2,24,128]{2,1,0:T(8,128)} %get-tuple-element.19.refs_0_), channel_id=1, source_target_pairs={{0,24},{8,32},{16,40},{24,48},{32,56},{40,64},{48,72},{56,80},{64,... | collective-permute-start | bytes 73736 | tf_op jit(solution)/shard_map/ppermute | solution.py:371
  56.4 1.9 %collective-permute-start.7 = (f32[2,24,128]{2,1,0:T(8,128)}, f32[2,24,128]{2,1,0:T(8,128)S(1)}, u32[]{:S(2)}, u32[]{:S(2)}) collective-permute-start(f32[2,24,128]{2,1,0:T(8,128)} %get-tuple-element.19.refs_0_), channel_id=1, source_target_pairs={{0,16},{8,24},{16,32},{24,40},{32,48},{40,56},{48,64},{56,72},{64,... | collective-permute-start | bytes 73736 | tf_op jit(solution)/shard_map/ppermute | solution.py:371
  58.4 2.5 %collective-permute-start.6 = (f32[2,24,128]{2,1,0:T(8,128)}, f32[2,24,128]{2,1,0:T(8,128)S(1)}, u32[]{:S(2)}, u32[]{:S(2)}) collective-permute-start(f32[2,24,128]{2,1,0:T(8,128)} %get-tuple-element.19.refs_0_), channel_id=1, source_target_pairs={{0,8},{8,16},{16,24},{24,32},{32,40},{40,48},{48,56},{56,64},{64,7... | collective-permute-start | bytes 73736 | tf_op jit(solution)/shard_map/ppermute | solution.py:371
  60.8 6.8 %collective-permute-done.8.refs_3_ = f32[2,24,128]{2,1,0:T(8,128)S(1)} collective-permute-done((f32[2,24,128]{2,1,0:T(8,128)}, f32[2,24,128]{2,1,0:T(8,128)S(1)}, u32[]{:S(2)}, u32[]{:S(2)}) %collective-permute-start.8) | collective-permute-done | bytes 24608 | tf_op jit(solution)/shard_map/ppermute | solution.py:371
  67.7 2.3 %collective-permute-done.7.refs_2_ = f32[2,24,128]{2,1,0:T(8,128)S(1)} collective-permute-done((f32[2,24,128]{2,1,0:T(8,128)}, f32[2,24,128]{2,1,0:T(8,128)S(1)}, u32[]{:S(2)}, u32[]{:S(2)}) %collective-permute-start.7) | collective-permute-done | bytes 24608 | tf_op jit(solution)/shard_map/ppermute | solution.py:371
  69.9 0.6 copy-done.4
  70.5 0.6 copy-done.5
  71.1 1.5 %unpack.1 = f32[5,6,512]{2,1,0:T(8,128)} custom-call(f32[2,24,128]{2,1,0:T(8,128)} %get-tuple-element.19.refs_0_, f32[2,24,128]{2,1,0:T(8,128)} %copy-done.5, f32[2,24,128]{2,1,0:T(8,128)} %copy-done.4, f32[2,24,128]{2,1,0:T(8,128)} %copy-done.3), custom_call_target="tpu_custom_call" | custom-call | tf_op jit(solution)/shard_map/unpack/pallas_call | solution.py:434
  (17 shorter events, 0.0 us)
Async XLA Ops:
  2.3 37.2 %collective-permute-start = (f32[2,16,128]{2,1,0:T(8,128)}, f32[2,16,128]{2,1,0:T(8,128)S(1)}, u32[]{:S(2)}, u32[]{:S(2)}) collective-permute-start(f32[2,16,128]{2,1,0:T(8,128)} %get-tuple-element.13), channel_id=1, source_target_pairs={{0,1},{1,0},{2,3},{3,2},{4,5},{5,4},{6,7},{7,6},{8,9},{9,8},{10,11... | collective-permute-start | bytes 49160 | tf_op jit(solution)/shard_map/ppermute | solution.py:409
  22.2 17.2 %collective-permute-start.1 = (f32[5,256]{1,0:T(8,128)}, f32[5,256]{1,0:T(8,128)S(1)}, u32[]{:S(2)}, u32[]{:S(2)}) collective-permute-start(f32[5,256]{1,0:T(8,128)} %get-tuple-element.14), channel_id=1, source_target_pairs={{0,8},{8,16},{16,24},{24,32},{32,40},{40,48},{48,56},{56,64},{64,7... | collective-permute-start | bytes 15368 | tf_op jit(solution)/shard_map/ppermute | solution.py:371
  26.2 21.0 %collective-permute-start.4 = (f32[6,24,128]{2,1,0:T(8,128)}, f32[6,24,128]{2,1,0:T(8,128)S(1)}, u32[]{:S(2)}, u32[]{:S(2)}) collective-permute-start(f32[6,24,128]{2,1,0:T(8,128)} %bitcast.6), channel_id=1, source_target_pairs={{0,1000},{8,1008},{16,1016},{24,0},{32,8},{40,16},{48,24},{56,32},... | collective-permute-start | bytes 221192 | tf_op jit(solution)/shard_map/ppermute | solution.py:371
  36.4 10.8 %collective-permute-start.3 = (f32[6,24,128]{2,1,0:T(8,128)}, f32[6,24,128]{2,1,0:T(8,128)S(1)}, u32[]{:S(2)}, u32[]{:S(2)}) collective-permute-start(f32[6,24,128]{2,1,0:T(8,128)} %bitcast.7), channel_id=1, source_target_pairs={{0,1008},{8,1016},{16,0},{24,8},{32,16},{40,24},{48,32},{56,40},{6... | collective-permute-start | bytes 221192 | tf_op jit(solution)/shard_map/ppermute | solution.py:371
  39.4 0.6 copy-start.8
  39.4 0.6 copy-start.7
  40.0 7.2 %collective-permute-start.5 = (f32[2,16,128]{2,1,0:T(8,128)}, f32[2,16,128]{2,1,0:T(8,128)S(1)}, u32[]{:S(2)}, u32[]{:S(2)}) collective-permute-start(f32[2,16,128]{2,1,0:T(8,128)} %get-tuple-element.16.pair_ref), channel_id=1, source_target_pairs={{0,2},{1,7},{2,4},{3,1},{4,6},{5,3},{6,0},{7,5},{8,10},{9,15},{10,... | collective-permute-start | bytes 49160 | tf_op jit(solution)/shard_map/ppermute | solution.py:415
  43.1 6.6 %collective-permute-start.2 = (f32[6,24,128]{2,1,0:T(8,128)}, f32[6,24,128]{2,1,0:T(8,128)S(1)}, u32[]{:S(2)}, u32[]{:S(2)}) collective-permute-start(f32[6,24,128]{2,1,0:T(8,128)} %bitcast.9), channel_id=1, source_target_pairs={{0,1016},{8,0},{16,8},{24,16},{32,24},{40,32},{48,40},{56,48},{64,... | collective-permute-start | bytes 221192 | tf_op jit(solution)/shard_map/ppermute | solution.py:371
  47.2 0.6 copy-start.6
  47.2 0.6 copy-start
  47.8 0.6 copy-start.1
  49.7 0.6 copy-start.2
  53.4 14.2 %collective-permute-start.8 = (f32[2,24,128]{2,1,0:T(8,128)}, f32[2,24,128]{2,1,0:T(8,128)S(1)}, u32[]{:S(2)}, u32[]{:S(2)}) collective-permute-start(f32[2,24,128]{2,1,0:T(8,128)} %get-tuple-element.19.refs_0_), channel_id=1, source_target_pairs={{0,24},{8,32},{16,40},{24,48},{32,56},{40,64},{48,72},{56,80},{64,... | collective-permute-start | bytes 73736 | tf_op jit(solution)/shard_map/ppermute | solution.py:371
  56.4 13.5 %collective-permute-start.7 = (f32[2,24,128]{2,1,0:T(8,128)}, f32[2,24,128]{2,1,0:T(8,128)S(1)}, u32[]{:S(2)}, u32[]{:S(2)}) collective-permute-start(f32[2,24,128]{2,1,0:T(8,128)} %get-tuple-element.19.refs_0_), channel_id=1, source_target_pairs={{0,16},{8,24},{16,32},{24,40},{32,48},{40,56},{48,64},{56,72},{64,... | collective-permute-start | bytes 73736 | tf_op jit(solution)/shard_map/ppermute | solution.py:371
  58.4 11.6 %collective-permute-start.6 = (f32[2,24,128]{2,1,0:T(8,128)}, f32[2,24,128]{2,1,0:T(8,128)S(1)}, u32[]{:S(2)}, u32[]{:S(2)}) collective-permute-start(f32[2,24,128]{2,1,0:T(8,128)} %get-tuple-element.19.refs_0_), channel_id=1, source_target_pairs={{0,8},{8,16},{16,24},{24,32},{32,40},{40,48},{48,56},{56,64},{64,7... | collective-permute-start | bytes 73736 | tf_op jit(solution)/shard_map/ppermute | solution.py:371
  67.7 2.3 %copy-start.3 = (f32[2,24,128]{2,1,0:T(8,128)}, f32[2,24,128]{2,1,0:T(8,128)S(1)}, u32[]{:S(2)}) copy-start(f32[2,24,128]{2,1,0:T(8,128)S(1)} %collective-permute-done.8.refs_3_) | copy-start | bytes 73732
  69.9 0.6 copy-start.4
  70.5 0.6 copy-start.5

commit v4 on v3

--- a/solution.py
+++ b/solution.py
@@ -375,16 +375,16 @@
     return pl.BlockSpec(memory_space=space)
 
 
-def in_order(*values):
+def in_order(value, *earlier):
     return pl.pallas_call(
         order_kernel,
-        out_shape=tuple(jax.ShapeDtypeStruct(value.shape, value.dtype) for value in values),
-        in_specs=[full(pl.ANY)] + [full(pltpu.HBM)] * (len(values) - 1),
-        out_specs=tuple([full(pl.ANY)] + [full(pltpu.HBM)] * (len(values) - 1)),
-        input_output_aliases={i: i for i in range(len(values))},
+        out_shape=jax.ShapeDtypeStruct(value.shape, value.dtype),
+        in_specs=[full(pl.ANY)] + [full(pltpu.HBM)] * len(earlier),
+        out_specs=full(pl.ANY),
+        input_output_aliases={0: 0},
         cost_estimate=pl.CostEstimate(flops=10**9, bytes_accessed=10**9, transcendentals=0),
         name="order",
-    )(*values)
+    )(value, *earlier)
 
 
 def body(coarse_state, fine_state, fine_anchor, fine_owner):
@@ -410,7 +410,7 @@
     z_before = moved_along(z_high, "node", 1)
     third = moved_along(slots, "node", -3)
     second = moved_along(slots, "node", -2)
-    later, pair, z_before = in_order(later, pair, z_before)
+    later = in_order(later, pair, z_before)
     later = later.reshape(CAP, SLOT_ROWS, 128)
     relay = lax.ppermute(pair, "dev", [(d, (d + 2 - 4 * (d % 2)) % devs) for d in range(devs)])
     token = pl.pallas_call(

time: 73.4 us -> 73.5 us (level)
  the two profiles are of different devices: /device:TPU:1 before, /device:TPU:2 now
where the time goes in v4:
time: 73.5 us; the launch traced here: 72.9 us
  starting transfers between devices  49.8 us (68%)
  waiting for transfers between devices  13 us (18%)
  Pallas kernels  6.23 us (8%)
  local copies, waits for them, and re-layouts  3.06 us (4%)
  between operations  0.79 us (1%)
    ppermute x7, starting transfers between devices, moved_along(): lax.ppermute(value, axis, [(i, (i + steps) % count) for i in range(count)])  27.1 us
    ppermute x1, starting transfers between devices, body(): pair = lax.ppermute(edges, 'dev', [(d, d ^ 1) for d in range(devs)])  19.3 us
    ppermute x7, waiting for transfers between devices, moved_along(): lax.ppermute(value, axis, [(i, (i + steps) % count) for i in range(count)])  13 us
    ppermute x1, starting transfers between devices, body(): lax.ppermute(pair, 'dev', [(d, (d + 2 - 4 * (d % 2)) % devs) for d in ran...  3.4 us
    pallas_call x1, Pallas kernels, body(): pl.pallas_call(step_kernel, out_shape=(like(5, B, ROW), like(2, SLOT_ROWS...  3.12 us
    unnamed x18, local copies, waits for them, and re-layouts  3.06 us
    pallas_call x1, Pallas kernels, body(): pl.pallas_call(pack_kernel, out_shape=(like(CAP * SLOT_ROWS, 128), like(C...  1.64 us
  transfers between devices with their start and end apart: 9, of which 4 were waited for; matrix products, arithmetic and copies ran while one was open for 0% of the time, Pallas kernels for 0%

profile of v4, /device:TPU:2, one launch (start us, length us, event | category | flops | bytes accessed | tf_op | source)
XLA Modules:
  0.0 72.9 jit_solution(10078709859971967001)
XLA Ops:
  0.6 1.6 %pack.1 = (f32[144,128]{1,0:T(8,128)}, f32[144,128]{1,0:T(8,128)}, f32[2,16,128]{2,1,0:T(8,128)}, f32[5,256]{1,0:T(8,128)}) custom-call(f32[5,16,256]{2,1,0:T(8,128)} %coarse_ref.3, f32[5,6,512]{2,1,0:T(8,128)} %bitcast.4), custom_call_target="tpu_custom_call" | custom-call | tf_op jit(solution)/shard_map/pack/pallas_call | solution.py:395
  2.3 19.3 %collective-permute-start = (f32[2,16,128]{2,1,0:T(8,128)}, f32[2,16,128]{2,1,0:T(8,128)S(1)}, u32[]{:S(2)}, u32[]{:S(2)}) collective-permute-start(f32[2,16,128]{2,1,0:T(8,128)} %get-tuple-element.10), channel_id=1, source_target_pairs={{0,1},{1,0},{2,3},{3,2},{4,5},{5,4},{6,7},{7,6},{8,9},{9,8},{10,11... | collective-permute-start | bytes 49160 | tf_op jit(solution)/shard_map/ppermute | solution.py:409
  21.6 1.9 %collective-permute-start.1 = (f32[5,256]{1,0:T(8,128)}, f32[5,256]{1,0:T(8,128)S(1)}, u32[]{:S(2)}, u32[]{:S(2)}) collective-permute-start(f32[5,256]{1,0:T(8,128)} %get-tuple-element.11), channel_id=1, source_target_pairs={{0,8},{8,16},{16,24},{24,32},{32,40},{40,48},{48,56},{56,64},{64,7... | collective-permute-start | bytes 15368 | tf_op jit(solution)/shard_map/ppermute | solution.py:371
  23.6 12.9 %collective-permute-start.4 = (f32[6,24,128]{2,1,0:T(8,128)}, f32[6,24,128]{2,1,0:T(8,128)S(1)}, u32[]{:S(2)}, u32[]{:S(2)}) collective-permute-start(f32[6,24,128]{2,1,0:T(8,128)} %bitcast.6), channel_id=1, source_target_pairs={{0,1000},{8,1008},{16,1016},{24,0},{32,8},{40,16},{48,24},{56,32},... | collective-permute-start | bytes 221192 | tf_op jit(solution)/shard_map/ppermute | solution.py:371
  36.5 3.3 %collective-permute-start.3 = (f32[6,24,128]{2,1,0:T(8,128)}, f32[6,24,128]{2,1,0:T(8,128)S(1)}, u32[]{:S(2)}, u32[]{:S(2)}) collective-permute-start(f32[6,24,128]{2,1,0:T(8,128)} %bitcast.7), channel_id=1, source_target_pairs={{0,1008},{8,1016},{16,0},{24,8},{32,16},{40,24},{48,32},{56,40},{6... | collective-permute-start | bytes 221192 | tf_op jit(solution)/shard_map/ppermute | solution.py:371
  39.7 0.0 collective-permute-done.refs_1_.pair_ref
  39.8 3.4 %collective-permute-start.5 = (f32[2,16,128]{2,1,0:T(8,128)S(1)}, f32[2,16,128]{2,1,0:T(8,128)S(1)}, u32[]{:S(2)}, u32[]{:S(2)}) collective-permute-start(f32[2,16,128]{2,1,0:T(8,128)S(1)} %collective-permute-done.refs_1_.pair_ref), channel_id=1, source_target_pairs={{0,2},{1,7},{2,4},{3,1},{4,6},{5,3},{6,0},{7,5},{8,10},{9,15},{10,... | collective-permute-start | bytes 49160 | tf_op jit(solution)/shard_map/ppermute | solution.py:415
  43.2 0.0 collective-permute-done.1.refs_2_.z_before_ref
  43.2 0.6 copy-done.8
  43.8 1.9 %collective-permute-start.2 = (f32[6,24,128]{2,1,0:T(8,128)}, f32[6,24,128]{2,1,0:T(8,128)S(1)}, u32[]{:S(2)}, u32[]{:S(2)}) collective-permute-start(f32[6,24,128]{2,1,0:T(8,128)} %bitcast.9), channel_id=1, source_target_pairs={{0,1016},{8,0},{16,8},{24,16},{32,24},{40,32},{48,40},{56,48},{64,... | collective-permute-start | bytes 221192 | tf_op jit(solution)/shard_map/ppermute | solution.py:371
  45.7 0.6 copy-done.7
  46.3 0.0 copy-done
  46.3 0.6 copy-done.1
  47.0 1.0 %collective-permute-done.2.one_ref = f32[6,24,128]{2,1,0:T(8,128)S(1)} collective-permute-done((f32[6,24,128]{2,1,0:T(8,128)}, f32[6,24,128]{2,1,0:T(8,128)S(1)}, u32[]{:S(2)}, u32[]{:S(2)}) %collective-permute-start.2) | collective-permute-done | bytes 73760 | tf_op jit(solution)/shard_map/ppermute | solution.py:371
  48.0 0.6 copy-done.2
  48.6 3.1 %step.1 = (f32[5,16,256]{2,1,0:T(8,128)}, f32[2,24,128]{2,1,0:T(8,128)}) custom-call(s32[1,2,3]{2,1,0:T(2,128)} %anchor_ref.1, s32[1,2,2]{2,1,0:T(2,128)} %owner_ref.1, f32[5,16,256]{2,1,0:T(8,128)} %coarse_ref.3, f32[6,24,128]{2,1,0:T(8,128)} %bitcast.8, f32[6,24,128]{2,1,0:T(8,128)} %copy-done.2, f32[6,24,128]{2,1,0:T(8,128)} %copy-done.1, ...), custom_call_target="tpu_custom_call" | custom-call | tf_op jit(solution)/shard_map/step/pallas_call | solution.py:425
  51.7 3.1 %collective-permute-start.8 = (f32[2,24,128]{2,1,0:T(8,128)}, f32[2,24,128]{2,1,0:T(8,128)S(1)}, u32[]{:S(2)}, u32[]{:S(2)}) collective-permute-start(f32[2,24,128]{2,1,0:T(8,128)} %get-tuple-element.13.refs_0_), channel_id=1, source_target_pairs={{0,24},{8,32},{16,40},{24,48},{32,56},{40,64},{48,72},{56,80},{64,... | collective-permute-start | bytes 73736 | tf_op jit(solution)/shard_map/ppermute | solution.py:371
  54.9 1.9 %collective-permute-start.7 = (f32[2,24,128]{2,1,0:T(8,128)}, f32[2,24,128]{2,1,0:T(8,128)S(1)}, u32[]{:S(2)}, u32[]{:S(2)}) collective-permute-start(f32[2,24,128]{2,1,0:T(8,128)} %get-tuple-element.13.refs_0_), channel_id=1, source_target_pairs={{0,16},{8,24},{16,32},{24,40},{32,48},{40,56},{48,64},{56,72},{64,... | collective-permute-start | bytes 73736 | tf_op jit(solution)/shard_map/ppermute | solution.py:371
  56.8 2.0 %collective-permute-start.6 = (f32[2,24,128]{2,1,0:T(8,128)}, f32[2,24,128]{2,1,0:T(8,128)S(1)}, u32[]{:S(2)}, u32[]{:S(2)}) collective-permute-start(f32[2,24,128]{2,1,0:T(8,128)} %get-tuple-element.13.refs_0_), channel_id=1, source_target_pairs={{0,8},{8,16},{16,24},{24,32},{32,40},{40,48},{48,56},{56,64},{64,7... | collective-permute-start | bytes 73736 | tf_op jit(solution)/shard_map/ppermute | solution.py:371
  58.8 8.1 %collective-permute-done.8.refs_3_ = f32[2,24,128]{2,1,0:T(8,128)S(1)} collective-permute-done((f32[2,24,128]{2,1,0:T(8,128)}, f32[2,24,128]{2,1,0:T(8,128)S(1)}, u32[]{:S(2)}, u32[]{:S(2)}) %collective-permute-start.8) | collective-permute-done | bytes 24608 | tf_op jit(solution)/shard_map/ppermute | solution.py:371
  66.9 2.6 %collective-permute-done.7.refs_2_ = f32[2,24,128]{2,1,0:T(8,128)S(1)} collective-permute-done((f32[2,24,128]{2,1,0:T(8,128)}, f32[2,24,128]{2,1,0:T(8,128)S(1)}, u32[]{:S(2)}, u32[]{:S(2)}) %collective-permute-start.7) | collective-permute-done | bytes 24608 | tf_op jit(solution)/shard_map/ppermute | solution.py:371
  69.5 1.4 %collective-permute-done.6.refs_1_ = f32[2,24,128]{2,1,0:T(8,128)S(1)} collective-permute-done((f32[2,24,128]{2,1,0:T(8,128)}, f32[2,24,128]{2,1,0:T(8,128)S(1)}, u32[]{:S(2)}, u32[]{:S(2)}) %collective-permute-start.6) | collective-permute-done | bytes 24608 | tf_op jit(solution)/shard_map/ppermute | solution.py:371
  70.9 0.6 copy-done.5
  71.5 1.5 %unpack.1 = f32[5,6,512]{2,1,0:T(8,128)} custom-call(f32[2,24,128]{2,1,0:T(8,128)} %get-tuple-element.13.refs_0_, f32[2,24,128]{2,1,0:T(8,128)} %copy-done.5, f32[2,24,128]{2,1,0:T(8,128)} %copy-done.4, f32[2,24,128]{2,1,0:T(8,128)} %copy-done.3), custom_call_target="tpu_custom_call" | custom-call | tf_op jit(solution)/shard_map/unpack/pallas_call | solution.py:434
  (17 shorter events, 0.0 us)
Async XLA Ops:
  2.3 37.5 %collective-permute-start = (f32[2,16,128]{2,1,0:T(8,128)}, f32[2,16,128]{2,1,0:T(8,128)S(1)}, u32[]{:S(2)}, u32[]{:S(2)}) collective-permute-start(f32[2,16,128]{2,1,0:T(8,128)} %get-tuple-element.10), channel_id=1, source_target_pairs={{0,1},{1,0},{2,3},{3,2},{4,5},{5,4},{6,7},{7,6},{8,9},{9,8},{10,11... | collective-permute-start | bytes 49160 | tf_op jit(solution)/shard_map/ppermute | solution.py:409
  21.6 21.5 %collective-permute-start.1 = (f32[5,256]{1,0:T(8,128)}, f32[5,256]{1,0:T(8,128)S(1)}, u32[]{:S(2)}, u32[]{:S(2)}) collective-permute-start(f32[5,256]{1,0:T(8,128)} %get-tuple-element.11), channel_id=1, source_target_pairs={{0,8},{8,16},{16,24},{24,32},{32,40},{40,48},{48,56},{56,64},{64,7... | collective-permute-start | bytes 15368 | tf_op jit(solution)/shard_map/ppermute | solution.py:371
  23.6 22.2 %collective-permute-start.4 = (f32[6,24,128]{2,1,0:T(8,128)}, f32[6,24,128]{2,1,0:T(8,128)S(1)}, u32[]{:S(2)}, u32[]{:S(2)}) collective-permute-start(f32[6,24,128]{2,1,0:T(8,128)} %bitcast.6), channel_id=1, source_target_pairs={{0,1000},{8,1008},{16,1016},{24,0},{32,8},{40,16},{48,24},{56,32},... | collective-permute-start | bytes 221192 | tf_op jit(solution)/shard_map/ppermute | solution.py:371
  36.5 9.3 %collective-permute-start.3 = (f32[6,24,128]{2,1,0:T(8,128)}, f32[6,24,128]{2,1,0:T(8,128)S(1)}, u32[]{:S(2)}, u32[]{:S(2)}) collective-permute-start(f32[6,24,128]{2,1,0:T(8,128)} %bitcast.7), channel_id=1, source_target_pairs={{0,1008},{8,1016},{16,0},{24,8},{32,16},{40,24},{48,32},{56,40},{6... | collective-permute-start | bytes 221192 | tf_op jit(solution)/shard_map/ppermute | solution.py:371
  39.7 3.4 %copy-start.6 = (f32[2,16,128]{2,1,0:T(8,128)}, f32[2,16,128]{2,1,0:T(8,128)S(1)}, u32[]{:S(2)}) copy-start(f32[2,16,128]{2,1,0:T(8,128)S(1)} %collective-permute-done.refs_1_.pair_ref) | copy-start | bytes 49156
  39.8 5.9 %collective-permute-start.5 = (f32[2,16,128]{2,1,0:T(8,128)S(1)}, f32[2,16,128]{2,1,0:T(8,128)S(1)}, u32[]{:S(2)}, u32[]{:S(2)}) collective-permute-start(f32[2,16,128]{2,1,0:T(8,128)S(1)} %collective-permute-done.refs_1_.pair_ref), channel_id=1, source_target_pairs={{0,2},{1,7},{2,4},{3,1},{4,6},{5,3},{6,0},{7,5},{8,10},{9,15},{10,... | collective-permute-start | bytes 49160 | tf_op jit(solution)/shard_map/ppermute | solution.py:415
  43.2 0.6 copy-start.8
  43.8 4.2 %collective-permute-start.2 = (f32[6,24,128]{2,1,0:T(8,128)}, f32[6,24,128]{2,1,0:T(8,128)S(1)}, u32[]{:S(2)}, u32[]{:S(2)}) collective-permute-start(f32[6,24,128]{2,1,0:T(8,128)} %bitcast.9), channel_id=1, source_target_pairs={{0,1016},{8,0},{16,8},{24,16},{32,24},{40,32},{48,40},{56,48},{64,... | collective-permute-start | bytes 221192 | tf_op jit(solution)/shard_map/ppermute | solution.py:371
  45.7 0.6 copy-start.7
  45.7 0.6 copy-start
  46.3 0.6 copy-start.1
  48.0 0.6 copy-start.2
  51.7 15.2 %collective-permute-start.8 = (f32[2,24,128]{2,1,0:T(8,128)}, f32[2,24,128]{2,1,0:T(8,128)S(1)}, u32[]{:S(2)}, u32[]{:S(2)}) collective-permute-start(f32[2,24,128]{2,1,0:T(8,128)} %get-tuple-element.13.refs_0_), channel_id=1, source_target_pairs={{0,24},{8,32},{16,40},{24,48},{32,56},{40,64},{48,72},{56,80},{64,... | collective-permute-start | bytes 73736 | tf_op jit(solution)/shard_map/ppermute | solution.py:371
  54.9 14.6 %collective-permute-start.7 = (f32[2,24,128]{2,1,0:T(8,128)}, f32[2,24,128]{2,1,0:T(8,128)S(1)}, u32[]{:S(2)}, u32[]{:S(2)}) collective-permute-start(f32[2,24,128]{2,1,0:T(8,128)} %get-tuple-element.13.refs_0_), channel_id=1, source_target_pairs={{0,16},{8,24},{16,32},{24,40},{32,48},{40,56},{48,64},{56,72},{64,... | collective-permute-start | bytes 73736 | tf_op jit(solution)/shard_map/ppermute | solution.py:371
  56.8 14.1 %collective-permute-start.6 = (f32[2,24,128]{2,1,0:T(8,128)}, f32[2,24,128]{2,1,0:T(8,128)S(1)}, u32[]{:S(2)}, u32[]{:S(2)}) collective-permute-start(f32[2,24,128]{2,1,0:T(8,128)} %get-tuple-element.13.refs_0_), channel_id=1, source_target_pairs={{0,8},{8,16},{16,24},{24,32},{32,40},{40,48},{48,56},{56,64},{64,7... | collective-permute-start | bytes 73736 | tf_op jit(solution)/shard_map/ppermute | solution.py:371
  66.9 4.0 %copy-start.3 = (f32[2,24,128]{2,1,0:T(8,128)}, f32[2,24,128]{2,1,0:T(8,128)S(1)}, u32[]{:S(2)}) copy-start(f32[2,24,128]{2,1,0:T(8,128)S(1)} %collective-permute-done.8.refs_3_) | copy-start | bytes 73732
  69.5 1.4 %copy-start.4 = (f32[2,24,128]{2,1,0:T(8,128)}, f32[2,24,128]{2,1,0:T(8,128)S(1)}, u32[]{:S(2)}) copy-start(f32[2,24,128]{2,1,0:T(8,128)S(1)} %collective-permute-done.7.refs_2_) | copy-start | bytes 73732
  70.9 0.6 copy-start.5
